TPU v7x, 512 devices: a whole 4x4x16 slice. The times are simulated.
512 devices in a mesh: layer: 8 (over y, core), uvrow: 64 (over z, x).
Axes of the slice: x: 4, y: 4, z: 16, core: 2. Of those that a mesh axis runs over, the one named last changes fastest.
Arguments:
- vis_values: float32 [32768, 2, 128], P(('layer', 'uvrow')), may hold values from -6 to 6
- vis_cell: int32 [32768, 128], P(('layer', 'uvrow')), may hold values from 0 to 3871
- vis_offset: int32 [32768, 128], P(('layer', 'uvrow')), may hold values from 0 to 63
- block_tile: int32 [32768, 1], P(('layer', 'uvrow')), may hold values from 0 to 15
- block_band: int32 [32768, 1], P(('layer', 'uvrow')), may hold values from 0 to 63; in each aligned block of 64 rows (0 to 63, 64 to 127, ...) at most 2 rows name the same one
- layer_w: float32 [8], replicated, may hold values from -300 to 300
Outputs:
- dirty_map: float32 [2048, 2048], P(('layer', 'uvrow'))
Inputs may be any that keep to these rules, and one draw needn't show every extreme that they name: `block_band`: among the 64 blocks of one device no band is named more than 2 times, and in every draw some device names some band exactly 2 times.
All inputs are finite; a program needn't handle non-finite values.
Results may differ from a plain program's by a relative error of at most 0.0003.
Values sent between devices are 32-bit elements; how exact they have to be, the bound alone decides.
A program may use at most 64 MiB of HBM per device.

v0:
```python
import math

import jax
import jax.numpy as jnp
from jax import lax
from jax.sharding import PartitionSpec as P

N = 2048
TW = 128
K = 8
OVS = 8
RADIX = 128


KERNEL_SIGMA = 1.45
FIELD_WIDTH = 0.6
TOP_PRECISION = lax.Precision.HIGHEST


def shifted(shard, axis, by):
    peers = lax.axis_size(axis)
    return lax.ppermute(shard, axis, [(i, (i + by) % peers) for i in range(peers)])


def kernel_taps(distance, fraction, support):
    centre = (support - 1) / 2.0
    inside = (distance >= 0) & (distance < support)
    offset = distance.astype(jnp.float32) - centre - fraction
    values = jnp.exp(-(offset * offset) / (2.0 * KERNEL_SIGMA * KERNEL_SIGMA))
    return jnp.where(inside, values, 0.0)


def screen_phase(pixel_rows, pixel_cols, layer_depth, length):
    half_length = length // 2
    first_coord = ((pixel_rows + half_length) % length - half_length).astype(jnp.float32) * (
        FIELD_WIDTH / length
    )
    second_coord = ((pixel_cols + half_length) % length - half_length).astype(jnp.float32) * (
        FIELD_WIDTH / length
    )
    radius = first_coord[..., None] * first_coord[..., None] + second_coord * second_coord
    depth_term = -radius / (1.0 + jnp.sqrt(1.0 - radius))
    return 2.0 * math.pi * layer_depth * depth_term


def phase_table(first_count, second_count, length):
    cross = (
        jnp.arange(first_count, dtype=jnp.int32)[:, None]
        * jnp.arange(second_count, dtype=jnp.int32)[None, :]
        % length
    )
    angle = cross.astype(jnp.float32) * (2.0 * math.pi / length)
    return (jnp.cos(angle), jnp.sin(angle))


def complex_product(pattern, left_re, left_im, right_re, right_im):
    real_part = jnp.einsum(pattern, left_re, right_re, precision=TOP_PRECISION) - jnp.einsum(
        pattern, left_im, right_im, precision=TOP_PRECISION
    )
    imag_part = jnp.einsum(pattern, left_re, right_im, precision=TOP_PRECISION) + jnp.einsum(
        pattern, left_im, right_re, precision=TOP_PRECISION
    )
    return (real_part, imag_part)


def transform_to_front(field_re, field_im, factor):
    row_count, length = field_re.shape
    outer_size = length // factor
    shaped_re = field_re.reshape(row_count, factor, outer_size)
    shaped_im = field_im.reshape(row_count, factor, outer_size)
    inner_cos, inner_sin = phase_table(factor, factor, factor)
    first_re, first_im = complex_product("rba,bk->rak", shaped_re, shaped_im, inner_cos, inner_sin)
    twist_cos, twist_sin = phase_table(outer_size, factor, length)
    turned_re = first_re * twist_cos - first_im * twist_sin
    turned_im = first_re * twist_sin + first_im * twist_cos
    outer_cos, outer_sin = phase_table(outer_size, outer_size, outer_size)
    final_re, final_im = complex_product("jn,rnk->jkr", outer_cos, outer_sin, turned_re, turned_im)
    return (final_re.reshape(length, row_count), final_im.reshape(length, row_count))


def transform_last(field_re, field_im, factor):
    leading = field_re.shape[:-1]
    length = field_re.shape[-1]
    item_count = math.prod(leading)
    outer_size = length // factor
    shaped_re = field_re.reshape(item_count, factor, outer_size)
    shaped_im = field_im.reshape(item_count, factor, outer_size)
    inner_cos, inner_sin = phase_table(factor, factor, factor)
    first_re, first_im = complex_product("mba,bk->mak", shaped_re, shaped_im, inner_cos, inner_sin)
    twist_cos, twist_sin = phase_table(outer_size, factor, length)
    turned_re = first_re * twist_cos - first_im * twist_sin
    turned_im = first_re * twist_sin + first_im * twist_cos
    outer_cos, outer_sin = phase_table(outer_size, outer_size, outer_size)
    final_re, final_im = complex_product("mnk,jn->mjk", turned_re, turned_im, outer_cos, outer_sin)
    return (final_re.reshape(leading + (length,)), final_im.reshape(leading + (length,)))


def per_device(vis_values, vis_cell, vis_offset, block_tile, block_band, layer_w):
    band_count = lax.axis_size("uvrow")
    layer_count = lax.axis_size("layer")
    blocks = vis_values.shape[0]
    block_share = vis_values.shape[2]
    capacity = max(2, 2 * blocks // band_count)
    slot_count = band_count * capacity
    band_rows = N // band_count
    extended = band_rows + K - 1
    col_span = TW - K + 1
    tile_count = N // TW
    band_ids = block_band[:, 0]
    matches = (band_ids[:, None] == jnp.arange(band_count, dtype=jnp.int32)[None, :]).astype(
        jnp.int32
    )
    earlier = jnp.cumsum(matches, axis=0) - matches
    position = band_ids * capacity + jnp.sum(earlier * matches, axis=1)
    packed = vis_cell * (OVS * OVS) + vis_offset
    send_values = jnp.zeros((slot_count, 2, block_share), jnp.float32).at[position].set(vis_values)
    send_codes = jnp.zeros((slot_count, block_share), jnp.int32).at[position].set(packed)
    send_tiles = jnp.zeros((slot_count,), jnp.int32).at[position].set(block_tile[:, 0] + 1)
    recv_values, recv_codes, recv_tiles = (
        lax.all_to_all(
            send_values.reshape(band_count, capacity, 2, block_share),
            "uvrow",
            split_axis=0,
            concat_axis=0,
            tiled=True,
        ),
        lax.all_to_all(
            send_codes.reshape(band_count, capacity, block_share),
            "uvrow",
            split_axis=0,
            concat_axis=0,
            tiled=True,
        ),
        lax.all_to_all(
            send_tiles.reshape(band_count, capacity),
            "uvrow",
            split_axis=0,
            concat_axis=0,
            tiled=True,
        ),
    )
    group_size = 32
    group_count = slot_count // group_size
    row_axis = jnp.arange(extended, dtype=jnp.int32)
    col_axis = jnp.arange(TW, dtype=jnp.int32)
    tile_axis = jnp.arange(tile_count, dtype=jnp.int32)

    def add_group(summed_grid_cells, pieces):
        group_values, group_codes, group_tiles = pieces
        cell_ids = group_codes // (OVS * OVS)
        offsets = group_codes % (OVS * OVS)
        row_in = cell_ids // col_span
        col_in = cell_ids % col_span
        row_frac = (offsets // OVS).astype(jnp.float32) / OVS
        col_frac = (offsets % OVS).astype(jnp.float32) / OVS
        row_taps = kernel_taps(
            row_axis[None, :, None] - row_in[:, None, :], row_frac[:, None, :], K
        )
        weight_applied_values = jnp.concatenate(
            [row_taps * group_values[:, 0:1, :], row_taps * group_values[:, 1:2, :]], axis=1
        )
        column_kernel_taps = kernel_taps(
            col_axis[None, None, :] - col_in[:, :, None], col_frac[:, :, None], K
        )
        partial_grid_value = jnp.einsum(
            "nyl,nlw->nyw", weight_applied_values, column_kernel_taps, precision=TOP_PRECISION
        )
        selected_option = (group_tiles[:, None] - 1 == tile_axis[None, :]).astype(jnp.float32)
        return (
            summed_grid_cells
            + jnp.einsum(
                "iw,iqo->qwo", selected_option, partial_grid_value, precision=TOP_PRECISION
            ),
            None,
        )

    start_grid = jnp.zeros((2 * extended, tile_count, TW), jnp.float32)
    flat_values = recv_values.reshape(slot_count, 2, block_share)
    flat_codes = recv_codes.reshape(slot_count, block_share)
    flat_tiles = recv_tiles.reshape(slot_count)
    summed_grid_cells = lax.scan(
        add_group,
        start_grid,
        (
            flat_values.reshape(group_count, group_size, 2, block_share),
            flat_codes.reshape(group_count, group_size, block_share),
            flat_tiles.reshape(group_count, group_size),
        ),
    )[0]
    summed_grid_cells = summed_grid_cells.reshape(2, extended, N)
    spill = shifted(summed_grid_cells[:, band_rows:, :], "uvrow", 1)
    own_rows = summed_grid_cells[:, :band_rows, :]
    merged = jnp.concatenate([own_rows[:, : K - 1, :] + spill, own_rows[:, K - 1 :, :]], axis=1)
    spec_re, spec_im = transform_to_front(merged[0], merged[1], RADIX)
    row_block = N // (layer_count * band_count)
    spectrum = jnp.stack([spec_re, spec_im]).reshape(
        2, layer_count, band_count, row_block, band_rows
    )
    own_layer = lax.axis_index("layer")
    own_band = lax.axis_index("uvrow")
    norm_scale = 1.0 / math.sqrt(blocks * block_share * layer_count * band_count)
    pixel_cols = jnp.arange(N, dtype=jnp.int32)
    received = lax.all_to_all(spectrum, "uvrow", split_axis=2, concat_axis=4, tiled=True)
    image_re, image_im = transform_last(received[0], received[1], RADIX)
    images = jnp.stack([image_re, image_im])
    layer_depth = lax.dynamic_index_in_dim(layer_w, own_layer, 0, keepdims=False)
    pixel_rows = (
        jnp.arange(layer_count, dtype=jnp.int32)[:, None] * (N // layer_count)
        + own_band * row_block
        + jnp.arange(row_block, dtype=jnp.int32)[None, :]
    )
    phases = screen_phase(pixel_rows, pixel_cols, layer_depth, N)
    layer_term = (
        images[0, :, 0] * jnp.cos(phases) - images[1, :, 0] * jnp.sin(phases)
    ) * norm_scale
    summed = lax.psum(layer_term, "layer")
    dirty_map = lax.dynamic_index_in_dim(summed, own_layer, 0, keepdims=False)
    return dirty_map


def solution(mesh):
    placed = (
        P(("layer", "uvrow"), None, None),
        P(("layer", "uvrow"), None),
        P(("layer", "uvrow"), None),
        P(("layer", "uvrow"), None),
        P(("layer", "uvrow"), None),
        P(),
    )
    return jax.shard_map(
        per_device,
        mesh=mesh,
        in_specs=placed,
        out_specs=P(("layer", "uvrow"), None),
        check_vma=False,
    )
```

profile of v0, /device:TPU:7, one launch (start us, length us, event | category | flops | bytes accessed | tf_op | source)
XLA Modules:
  0.0 266.8 jit_solution(645997654953332489)
XLA Ops:
  10.4 18.0 %all-to-all-start.2 = ((s32[64,1,2]{2,1,0:T(1,128)}), s32[64,1,2]{2,1,0:T(1,128)S(1)}, u32[]{:S(2)}, u32[]{:S(2)}) async-start(s32[64,1,2]{2,1,0:T(1,128)} %bitcast.9), calls=%async_computation.2 | async-start | bytes 65536 | tf_op jit(solution)/shard_map/all_to_all | solution.py:134
  28.5 4.4 %scatter_fusion = f32[128,2,128]{2,1,0:T(2,128)S(1)} fusion(f32[128,2,128]{2,1,0:T(2,128)S(1)} %broadcast_in_dim.34, s32[64]{0:T(128)S(1)} %get-tuple-element.216, f32[64,2,128]{2,1,0:T(2,128)} %param.8), kind=kCustom, calls=%fused_computation.1 | custom fusion | bytes 196864 | tf_op jit(solution)/shard_map/scatter | solution.py:116
  33.6 6.6 %all-to-all-done.2 = s32[64,1,2]{2,1,0:T(1,128)S(1)} async-done(((s32[64,1,2]{2,1,0:T(1,128)}), s32[64,1,2]{2,1,0:T(1,128)S(1)}, u32[]{:S(2)}, u32[]{:S(2)}) %all-to-all-start.2) | async-done | bytes 544 | tf_op jit(solution)/shard_map/all_to_all | solution.py:134
  40.2 7.9 %all-to-all-start.1 = ((f32[64,2,2,128]{3,1,2,0:T(2,128)}), f32[64,2,2,128]{3,1,2,0:T(2,128)S(1)}, u32[]{:S(2)}, u32[]{:S(2)}) async-start(f32[64,2,2,128]{3,1,2,0:T(2,128)} %copy.58), calls=%async_computation.1 | async-start | bytes 262144 | tf_op jit(solution)/shard_map/all_to_all | solution.py:120
  49.7 12.2 %all-to-all-done.1 = f32[64,2,2,128]{3,1,2,0:T(2,128)S(1)} async-done(((f32[64,2,2,128]{3,1,2,0:T(2,128)}), f32[64,2,2,128]{3,1,2,0:T(2,128)S(1)}, u32[]{:S(2)}, u32[]{:S(2)}) %all-to-all-start.1) | async-done | bytes 131104 | tf_op jit(solution)/shard_map/all_to_all | solution.py:120
  61.9 7.5 %all-to-all-start = ((s32[64,2,128]{2,1,0:T(2,128)}), s32[64,2,128]{2,1,0:T(2,128)S(1)}, u32[]{:S(2)}, u32[]{:S(2)}) async-start(s32[64,2,128]{2,1,0:T(2,128)} %bitcast.4), calls=%async_computation | async-start | bytes 131072 | tf_op jit(solution)/shard_map/all_to_all | solution.py:127
  70.9 11.0 %all-to-all-done = s32[64,2,128]{2,1,0:T(2,128)S(1)} async-done(((s32[64,2,128]{2,1,0:T(2,128)}), s32[64,2,128]{2,1,0:T(2,128)S(1)}, u32[]{:S(2)}, u32[]{:S(2)}) %all-to-all-start) | async-done | bytes 65568 | tf_op jit(solution)/shard_map/all_to_all | solution.py:127
  81.8 24.0 %while.14 = (s32[]{:T(128)}, f32[78,16,128]{2,1,0:T(8,128)S(1)}, s32[4,32,128]{2,1,0:T(8,128)S(1)}, f32[4,32,2,128]{3,1,0,2:T(8,128)S(1)}, s32[4,32]{1,0:T(4,128)S(1)}, /*index=5*/s32[]{:T(128)}, s32[]{:T(128)}) while((s32[]{:T(128)}, f32[78,16,128]{2,1,0:T(8,128)S(1)}, s32[4,32,128]{2,1,0:T(8,128)S(1)}, ...), condition=%wide.region_6.7_spmd.clone, body=%wide.region_5.6_spmd.clone.sunk | while | flops 560869888 | bytes 6746611 | solution.py:181
  82.3 4.4 %fusion.255 = f32[32,78,128]{2,1,0:T(8,128)S(1)} fusion(f32[32,39,128]{2,1,0:T(8,128)S(1)} %get-tuple-element.263, f32[32,39,128]{2,1,0:T(8,128)S(1)} %get-tuple-element.264, f32[32,128]{1,0:T(8,128)S(1)} %get-tuple-element.265, s32[32,128]{1,0:T(8,128)S(1)} %get-tuple-element.266), kind=kOutput, calls=%fused_computation.17.clone.1 | convolution fusion | flops 496820224 | bytes 2588672 | tf_op jit(solution)/shard_map/while/body/eval_jaxpr/nyl,nlw->nyw/dot_general | solution.py:165
  88.3 4.4 %fusion.255 = f32[32,78,128]{2,1,0:T(8,128)S(1)} fusion(f32[32,39,128]{2,1,0:T(8,128)S(1)} %get-tuple-element.263, f32[32,39,128]{2,1,0:T(8,128)S(1)} %get-tuple-element.264, f32[32,128]{1,0:T(8,128)S(1)} %get-tuple-element.265, s32[32,128]{1,0:T(8,128)S(1)} %get-tuple-element.266), kind=kOutput, calls=%fused_computation.17.clone.1 | convolution fusion | flops 496820224 | bytes 2588672 | tf_op jit(solution)/shard_map/while/body/eval_jaxpr/nyl,nlw->nyw/dot_general | solution.py:165
  94.3 4.4 %fusion.255 = f32[32,78,128]{2,1,0:T(8,128)S(1)} fusion(f32[32,39,128]{2,1,0:T(8,128)S(1)} %get-tuple-element.263, f32[32,39,128]{2,1,0:T(8,128)S(1)} %get-tuple-element.264, f32[32,128]{1,0:T(8,128)S(1)} %get-tuple-element.265, s32[32,128]{1,0:T(8,128)S(1)} %get-tuple-element.266), kind=kOutput, calls=%fused_computation.17.clone.1 | convolution fusion | flops 496820224 | bytes 2588672 | tf_op jit(solution)/shard_map/while/body/eval_jaxpr/nyl,nlw->nyw/dot_general | solution.py:165
  100.3 4.4 %fusion.255 = f32[32,78,128]{2,1,0:T(8,128)S(1)} fusion(f32[32,39,128]{2,1,0:T(8,128)S(1)} %get-tuple-element.263, f32[32,39,128]{2,1,0:T(8,128)S(1)} %get-tuple-element.264, f32[32,128]{1,0:T(8,128)S(1)} %get-tuple-element.265, s32[32,128]{1,0:T(8,128)S(1)} %get-tuple-element.266), kind=kOutput, calls=%fused_computation.17.clone.1 | convolution fusion | flops 496820224 | bytes 2588672 | tf_op jit(solution)/shard_map/while/body/eval_jaxpr/nyl,nlw->nyw/dot_general | solution.py:165
  106.0 4.3 %collective-permute-start = (f32[2,7,2048]{2,1,0:T(8,128)S(1)}, f32[2,7,2048]{2,1,0:T(8,128)S(1)}, u32[]{:S(2)}, u32[]{:S(2)}) collective-permute-start(f32[2,7,2048]{2,1,0:T(8,128)S(1)} %slice.52), channel_id=1, source_target_pairs={{0,1},{1,2},{2,3},{3,4},{4,5},{5,6},{6,7},{7,8},{8,9},{9,10},{10,1... | collective-permute-start | bytes 344072 | tf_op jit(solution)/shard_map/ppermute | solution.py:22
  119.7 1.8 copy_bitcast_fusion
  121.5 2.1 reshape.329
  123.6 9.1 %all-to-all-start.3 = ((f32[64,1,2048]{2,1,0:T(1,128)}), f32[64,1,2048]{2,1,0:T(1,128)S(1)}, u32[]{:S(2)}, u32[]{:S(2)}) async-start(f32[64,1,2048]{2,1,0:T(1,128)} %reshape.329), calls=%async_computation.3 | async-start | bytes 1048576 | tf_op jit(solution)/shard_map/all_to_all | solution.py:203
  134.3 26.5 %all-to-all-done.3 = f32[64,1,2048]{2,1,0:T(1,128)S(1)} async-done(((f32[64,1,2048]{2,1,0:T(1,128)}), f32[64,1,2048]{2,1,0:T(1,128)S(1)}, u32[]{:S(2)}, u32[]{:S(2)}) %all-to-all-start.3) | async-done | bytes 524320 | tf_op jit(solution)/shard_map/all_to_all | solution.py:203
  161.3 1.9 reduce.4
  166.6 3.4 %fusion.88 = f32[32,16,128]{2,1,0:T(8,128)S(1)} fusion(f32[32,128,16]{2,1,0:T(8,128)S(1)} %reshape_squeeze.14), kind=kOutput, calls=%fused_computation.127 | convolution fusion | flops 100892672 | bytes 524288 | tf_op jit(solution)/shard_map/mba,bk->mak/dot_general | solution.py:60
  170.0 4.1 %fusion.95 = f32[32,16,128]{2,1,0:T(8,128)} fusion(f32[32,128,16]{2,1,0:T(8,128)S(1)} %reshape_squeeze.14), kind=kOutput, calls=%fused_computation.134 | convolution fusion | flops 100892672 | bytes 524288 | tf_op jit(solution)/shard_map/mba,bk->mak/dot_general | solution.py:57
  175.0 4.3 %convolution_subtract_fusion.1 = f32[32,16,128]{2,1,0:T(8,128)S(1)} fusion(f32[32,16,128]{2,1,0:T(8,128)} %fusion.95, f32[32,128,16]{2,1,0:T(8,128)S(1)} %reshape_squeeze.15), kind=kOutput, calls=%fused_computation.94 | convolution fusion | flops 100958208 | bytes 786432 | tf_op jit(solution)/shard_map/mba,bk->mak/dot_general | solution.py:57
  179.4 3.7 %convolution_add_fusion.1 = f32[32,16,128]{2,1,0:T(8,128)S(1)} fusion(f32[32,16,128]{2,1,0:T(8,128)S(1)} %fusion.88, f32[32,128,16]{2,1,0:T(8,128)S(1)} %reshape_squeeze.15), kind=kOutput, calls=%fused_computation.93 | convolution fusion | flops 100958208 | bytes 786432 | tf_op jit(solution)/shard_map/mba,bk->mak/dot_general | solution.py:60
  184.9 3.2 %subtract_multiply_fusion = f32[8,4,2048]{2,1,0:T(4,128)} fusion(f32[8,4,2048]{2,1,0:T(4,128)S(1)} %squeeze_stack_reshape.7, f32[8,4,2048]{2,1,0:T(4,128)S(1)} %squeeze_stack_reshape.6, f32[2048]{0:T(1024)S(1)} %fusion.129, f32[8,4]{1,0:T(8,128)S(1)} %fusion.151, f32[]{:T(128)} %bitcast.23), kind=kLoop, calls=%fused_computation.111 | loop fusion | flops 655360 | bytes 794756 | tf_op jit(solution)/shard_map/mul | solution.py:213
  188.1 70.5 %all-reduce.2.cloned.1.call-done = f32[8,4,2048]{2,1,0:T(4,128)} async-done(((f32[8,4,2048]{2,1,0:T(4,128)}), f32[8,4,2048]{2,1,0:T(4,128)}) %all-reduce.2.cloned.1.call-update) | async-done | bytes 262160 | tf_op jit(solution)/shard_map/psum | solution.py:216
  (92 shorter events, 31.9 us)
Async XLA Ops:
  10.4 29.8 %all-to-all-start.2 = ((s32[64,1,2]{2,1,0:T(1,128)}), s32[64,1,2]{2,1,0:T(1,128)S(1)}, u32[]{:S(2)}, u32[]{:S(2)}) async-start(s32[64,1,2]{2,1,0:T(1,128)} %bitcast.9), calls=%async_computation.2 | async-start | bytes 65536 | tf_op jit(solution)/shard_map/all_to_all | solution.py:134
  40.2 21.7 %all-to-all-start.1 = ((f32[64,2,2,128]{3,1,2,0:T(2,128)}), f32[64,2,2,128]{3,1,2,0:T(2,128)S(1)}, u32[]{:S(2)}, u32[]{:S(2)}) async-start(f32[64,2,2,128]{3,1,2,0:T(2,128)} %copy.58), calls=%async_computation.1 | async-start | bytes 262144 | tf_op jit(solution)/shard_map/all_to_all | solution.py:120
  61.9 19.9 %all-to-all-start = ((s32[64,2,128]{2,1,0:T(2,128)}), s32[64,2,128]{2,1,0:T(2,128)S(1)}, u32[]{:S(2)}, u32[]{:S(2)}) async-start(s32[64,2,128]{2,1,0:T(2,128)} %bitcast.4), calls=%async_computation | async-start | bytes 131072 | tf_op jit(solution)/shard_map/all_to_all | solution.py:127
  106.0 6.1 %collective-permute-start = (f32[2,7,2048]{2,1,0:T(8,128)S(1)}, f32[2,7,2048]{2,1,0:T(8,128)S(1)}, u32[]{:S(2)}, u32[]{:S(2)}) collective-permute-start(f32[2,7,2048]{2,1,0:T(8,128)S(1)} %slice.52), channel_id=1, source_target_pairs={{0,1},{1,2},{2,3},{3,4},{4,5},{5,6},{6,7},{7,8},{8,9},{9,10},{10,1... | collective-permute-start | bytes 344072 | tf_op jit(solution)/shard_map/ppermute | solution.py:22
  121.5 11.5 %copy-start.1 = (f32[8]{0:T(128)S(1)}, f32[8]{0:T(128)}, u32[]{:S(2)}) copy-start(f32[8]{0:T(128)} %param.13) | copy-start | bytes 100
  123.6 37.2 %all-to-all-start.3 = ((f32[64,1,2048]{2,1,0:T(1,128)}), f32[64,1,2048]{2,1,0:T(1,128)S(1)}, u32[]{:S(2)}, u32[]{:S(2)}) async-start(f32[64,1,2048]{2,1,0:T(1,128)} %reshape.329), calls=%async_computation.3 | async-start | bytes 1048576 | tf_op jit(solution)/shard_map/all_to_all | solution.py:203
  132.7 125.9 %all-reduce.2.cloned.1.call-start = ((), (), s32[]{:S(2)}) async-start(), calls=%async_computation.4 | async-start | bytes 524288 | tf_op jit(solution)/shard_map/psum | solution.py:216
  166.6 7.5 %copy-start = (f32[1,8,1,4,64,32]{5,3,1,0,4,2:T(4,128)S(1)}, f32[1,8,1,4,64,32]{5,3,1,0,4,2:T(4,128)}, u32[]{:S(2)}) copy-start(f32[1,8,1,4,64,32]{5,3,1,0,4,2:T(4,128)} %get-tuple-element.212) | copy-start | bytes 786436
Sparse Core Ops, SparseCore 0:
  188.3 70.2 all-reduce.1
where the time goes:
time: 270 us; the launch traced here: 267 us
  waiting for transfers between devices  128 us (47%)
  starting transfers between devices  47.1 us (17%)
  matrix products  43.2 us (16%)
  local copies, waits for them, and re-layouts  20 us (7%)
  between operations  14.4 us (5%)
  other arithmetic  13.4 us (5%)
    psum x1, waiting for transfers between devices, per_device(): summed = lax.psum(layer_term, 'layer')  70.5 us
    all_to_all x1, waiting for transfers between devices, per_device(): lax.all_to_all(spectrum, 'uvrow', split_axis=2, concat_axis=4, tiled=True)  26.5 us
    all_to_all x1, starting transfers between devices, per_device(): lax.all_to_all(send_tiles.reshape(band_count, capacity), 'uvrow', split_a...  18 us
    dot_general x4, matrix products, add_group(): jnp.einsum('nyl,nlw->nyw', weight_applied_values, column_kernel_taps, pre...  17.8 us
    all_to_all x1, waiting for transfers between devices, per_device(): lax.all_to_all(send_values.reshape(band_count, capacity, 2, block_share),...  12.2 us
    all_to_all x1, waiting for transfers between devices, per_device(): lax.all_to_all(send_codes.reshape(band_count, capacity, block_share), 'uv...  11 us
    all_to_all x1, starting transfers between devices, per_device(): lax.all_to_all(spectrum, 'uvrow', split_axis=2, concat_axis=4, tiled=True)  9.07 us
    all_to_all x1, starting transfers between devices, per_device(): lax.all_to_all(send_values.reshape(band_count, capacity, 2, block_share),...  7.93 us
  transfers between devices with their start and end apart: 6, of which 6 were waited for; matrix products, arithmetic and copies ran while one was open for 3% of the time, Pallas kernels for 0%

commit v1 on v0

v1 whole, which is shorter than its diff:
```python
import functools
import math

import jax
import jax.numpy as jnp
import ml_dtypes
import numpy as np
from jax import lax
from jax.experimental import pallas as pl
from jax.experimental.pallas import tpu as pltpu
from jax.sharding import PartitionSpec as P

N = 2048
TW = 128
K = 8
SPAN = TW - K + 1
BANDS = 64
LAYERS = 8
BLOCKS = 64
ROWS = 32
EXT = 40
SIGMA = 1.45
WIDTH = 0.6
TAP_SCALE = math.sqrt(math.log2(math.e) / (2.0 * SIGMA * SIGMA))
MESH = pl.DeviceIdType.MESH
F32 = jnp.float32
BF16 = jnp.bfloat16
NN = (((1,), (0,)), ((), ()))
NT = (((1,), (1,)), ((), ()))


def halves(x):
    high = x.astype(BF16)
    low = (x - high.astype(F32)).astype(BF16)
    return high, low


def host_halves(x):
    high = x.astype(np.float32).astype(ml_dtypes.bfloat16)
    low = (x - high.astype(np.float64)).astype(np.float32).astype(ml_dtypes.bfloat16)
    return high, low


def host_tables():
    p1 = np.array([16 * k + z for z in range(16) for k in range(8)])
    col = np.arange(TW)
    angle = 2 * np.pi * ((p1[:, None] * col[None, :]) % TW) / TW
    high, low = host_halves(np.concatenate([np.cos(angle), np.sin(angle)], axis=1))
    outer = np.concatenate([high, high, low], axis=1)
    angle = 2 * np.pi * (np.arange(16)[:, None] * col[None, :]) / N
    twist = np.stack([np.cos(angle), np.sin(angle)]).astype(np.float32)
    q0 = np.arange(64)
    angle = 2 * np.pi * ((q0[:, None] * q0[None, :]) % 64) / 64
    high, low = host_halves(np.concatenate([np.cos(angle), np.sin(angle)], axis=0))
    bands = np.concatenate([high, high, low], axis=1)
    r = np.arange(ROWS)
    angle = 2 * np.pi * (q0[:, None] * r[None, :]) / N
    cos, sin = np.cos(angle), np.sin(angle)
    turn = np.stack(
        [np.concatenate([cos, -sin] * 2, axis=1), np.concatenate([sin, cos] * 2, axis=1)]
    ).astype(np.float32)
    angle = 2 * np.pi * ((r[:, None] * r[None, :]) % ROWS) / ROWS
    cos, sin = np.cos(angle), np.sin(angle)
    last = np.zeros((2, 2, 2, 2, ROWS, 2, 4, ROWS))
    for ih in range(2):
        for il in range(2):
            for c in range(2):
                last[ih, 0, il, c, :, 0, 2 * ih + il, :] = cos
                last[ih, 0, il, c, :, 1, 2 * ih + il, :] = sin
                last[ih, 1, il, c, :, 0, 2 * ih + il, :] = -sin
                last[ih, 1, il, c, :, 1, 2 * ih + il, :] = cos
    high, low = host_halves(last.reshape(2, 256, 256))
    final = np.concatenate([high, high, low], axis=1)
    return outer, twist, bands, turn, final


def cos_sin_turns(turns):
    quarters = turns * 4.0
    whole = jnp.round(quarters)
    t = (quarters - whole) * (math.pi / 2)
    s = t * t
    sin = t + t * s * (-1.6666654611e-1 + s * (8.3321608736e-3 - s * 1.9515295891e-4))
    cos = 1.0 - 0.5 * s + s * s * (4.166664568298827e-2 + s * (-1.388731625493765e-3 + s * 2.443315711809948e-5))
    n = whole.astype(jnp.int32)
    odd = (n & 1) == 1
    a = jnp.where(odd, sin, cos)
    b = jnp.where(odd, cos, sin)
    a = jnp.where(((n + 1) & 2) == 2, -a, a)
    b = jnp.where((n & 2) == 2, -b, b)
    return a, b


def wrapped(pixel):
    return (((pixel + N // 2) & (N - 1)) - N // 2).astype(F32) * (WIDTH / N)


def kernel(
    values, cell, offset, tile, band, depth_ref,
    outer, twist, bands, turn, final, out,
    vis_send, vis_recv, parts, tiles, spec, spill, col_send, col_recv, screen, red_send, red_recv,
    vis_ssem, vis_rsem, spill_ssem, spill_rsem, col_ssem, col_rsem, red_ssem, red_rsem,
):
    g, w = lax.axis_index("layer"), lax.axis_index("uvrow")
    z, x = w >> 2, w & 3

    barrier = pltpu.get_barrier_semaphore()

    @pl.loop(1, BANDS)
    def _(i):
        pl.semaphore_signal(barrier, inc=1, device_id={"layer": g, "uvrow": w ^ i}, device_id_type=MESH)

    @pl.loop(1, LAYERS)
    def _(i):
        pl.semaphore_signal(barrier, inc=1, device_id={"layer": g ^ i, "uvrow": w}, device_id_type=MESH)

    row_id = lax.broadcasted_iota(jnp.int32, (BLOCKS, BLOCKS), 0)
    col_id = lax.broadcasted_iota(jnp.int32, (BLOCKS, BLOCKS), 1)
    own = jnp.broadcast_to(band[...], (BLOCKS, BLOCKS))
    other = jnp.sum(jnp.where(row_id == col_id, own, 0), axis=0, keepdims=True)
    same = own == other
    rank = jnp.sum(jnp.where(same & (row_id < col_id), 1, 0), axis=0, keepdims=True)
    cells = cell[...].astype(F32)
    rows = jnp.floor((cells + 0.5) * (1.0 / SPAN))
    cols = cells - rows * SPAN
    shifts = offset[...]
    u_place = rows * 8.0 + (shifts >> 3).astype(F32)
    v_place = (cols + tile[...].astype(F32) * TW) * 8.0 + (shifts & 7).astype(F32)
    data = jnp.concatenate([values[:, 0, :], values[:, 1, :], u_place, v_place], axis=1)
    first = data.astype(BF16)
    rest = data - first.astype(F32)
    second = rest.astype(BF16)
    third = (rest - second.astype(F32)).astype(BF16)
    stacked = jnp.concatenate([first, second, third], axis=0)
    for j in range(2):
        pick = jnp.where((row_id == other) & (rank == j), 1.0, 0.0).astype(BF16)
        pick = jnp.concatenate([pick, pick, pick], axis=1)
        slots = lax.dot_general(pick, stacked, NN, preferred_element_type=F32)
        for f in range(4):
            vis_send[pl.ds(4 * j + f, BANDS, stride=8), :] = slots[:, f * 128 : (f + 1) * 128]

    depth = depth_ref[g]
    lane = lax.broadcasted_iota(jnp.int32, (64, 128), 1)
    y = wrapped((lane & 31) * 64 + lax.broadcasted_iota(jnp.int32, (64, 128), 0))

    @pl.loop(0, LAYERS)
    def _(k):
        xp = wrapped(256 * k + 4 * w + (lane >> 5))
        r = xp * xp + y * y
        turns = depth * (-r / (1.0 + jnp.sqrt(1.0 - r)))
        cos, sin = cos_sin_turns(turns)
        screen[k, 0] = cos * (1.0 / N)
        screen[k, 1] = sin * (1.0 / N)

    pl.semaphore_wait(barrier, BANDS - 1 + LAYERS - 1)

    def vis_copy(i):
        there = w ^ i
        return pltpu.make_async_remote_copy(
            src_ref=vis_send.at[pl.ds(pl.multiple_of(there * 8, 8), 8)],
            dst_ref=vis_recv.at[pl.ds(pl.multiple_of(w * 8, 8), 8)],
            send_sem=vis_ssem,
            recv_sem=vis_rsem.at[i],
            device_id={"layer": g, "uvrow": there},
            device_id_type=MESH,
        )

    @pl.loop(1, BANDS)
    def _(i):
        vis_copy(i).start()

    mine = pl.ds(pl.multiple_of(w * 8, 8), 8)
    vis_recv[mine, :] = vis_send[mine, :]

    row_axis = lax.broadcasted_iota(jnp.int32, (EXT, 128), 0).astype(F32)
    col_axis = lax.broadcasted_iota(jnp.int32, (TW, 128), 0).astype(F32)

    def taps(axis, place):
        begin = jnp.floor(place * 0.125)
        far = axis * TAP_SCALE - (place * 0.125 + (K - 1) / 2.0) * TAP_SCALE
        inside = (axis >= begin) & (axis < begin + K)
        return jnp.where(inside, jnp.exp2(-(far * far)), 0.0)

    @pl.loop(0, BANDS)
    def _(i):
        there = pl.multiple_of((w ^ i) * 8, 8)

        @pl.when(i > 0)
        def _():
            piece = vis_recv.at[pl.ds(there, 8)]
            pltpu.make_async_copy(piece, piece, vis_rsem.at[i]).wait()

        message = vis_recv[pl.ds(there, 8), :]
        for j in range(2):
            v_all = message[4 * j + 3 : 4 * j + 4]
            number = jnp.floor(v_all * (1.0 / 1024))
            row_taps = taps(row_axis, message[4 * j + 2 : 4 * j + 3])
            weighted = jnp.concatenate(
                [row_taps * message[4 * j : 4 * j + 1], row_taps * message[4 * j + 1 : 4 * j + 2]], axis=0
            )
            col_taps = taps(col_axis, v_all - number * 1024.0)
            wh, wl = halves(weighted)
            ch, cl = halves(col_taps)
            patch = lax.dot_general(
                jnp.concatenate([wh, wl, wh], axis=1),
                jnp.concatenate([ch, ch, cl], axis=1),
                NT,
                preferred_element_type=F32,
            )
            parts[pl.ds(pl.multiple_of((2 * i + j) * 2 * EXT, 16), 2 * EXT), :] = patch
            tiles[pl.ds(2 * i + j, 1), :] = number

    by_slot = jnp.transpose(tiles[...])[:16]
    p0 = lax.broadcasted_iota(jnp.int32, (16, 128), 0).astype(F32)
    cos, sin = cos_sin_turns(by_slot * p0 * (1.0 / 16))
    mh, ml = halves(jnp.concatenate([cos, sin], axis=0))
    mix = jnp.concatenate([mh, mh, ml], axis=1)

    def tile_row(u):
        re = parts[pl.ds(u, 128, stride=2 * EXT), :]
        im = parts[pl.ds(u + EXT, 128, stride=2 * EXT), :]
        ph, plo = halves(jnp.concatenate([re, im], axis=1))
        both = lax.dot_general(
            mix, jnp.concatenate([ph, plo, ph], axis=0), NN, preferred_element_type=F32
        )
        re = both[:16, :128] - both[16:, 128:]
        im = both[:16, 128:] + both[16:, :128]
        tc, ts = twist[0], twist[1]
        at = pl.ds(pl.multiple_of(u * 16, 16), 16)
        spec[0, at, :] = re * tc - im * ts
        spec[1, at, :] = re * ts + im * tc

    @pl.loop(ROWS, EXT)
    def _(u):
        tile_row(u)

    after, before = (w + 1) & (BANDS - 1), (w + BANDS - 1) & (BANDS - 1)
    spill_copy = pltpu.make_async_remote_copy(
        src_ref=spec.at[:, pl.ds(ROWS * 16, (EXT - ROWS) * 16)],
        dst_ref=spill,
        send_sem=spill_ssem,
        recv_sem=spill_rsem,
        device_id={"layer": g, "uvrow": after},
        device_id_type=MESH,
    )
    spill_copy.start()

    @pl.loop(0, ROWS)
    def _(u):
        tile_row(u)

    spill_copy.wait()
    over = pl.ds(0, (EXT - ROWS) * 16)
    spec[:, over, :] = spec[:, over, :] + spill[...]

    for pair in range(8):
        there_x, ih = pair // 2, pair % 2
        operand = []
        for il in range(2):
            re = spec[0, pl.ds(2 * pair + il, ROWS, stride=16), :]
            im = spec[1, pl.ds(2 * pair + il, ROWS, stride=16), :]
            operand.append(jnp.concatenate([re, -im], axis=1))
            operand.append(jnp.concatenate([im, re], axis=1))
        oh, ol = halves(jnp.concatenate(operand, axis=0))
        half = lax.dot_general(
            outer[...], jnp.concatenate([oh, ol, oh], axis=1), NT, preferred_element_type=F32
        )
        for there_z in range(16):
            at = (4 * there_z + there_x) * 16 + 8 * ih
            col_send[at : at + 8, :] = half[8 * there_z : 8 * there_z + 8]
        if ih == 1:

            @pl.loop(0, 16)
            def _(dz):
                there = ((z ^ dz) << 2) + there_x

                @pl.when(there != w)
                def _():
                    pltpu.make_async_remote_copy(
                        src_ref=col_send.at[pl.ds(pl.multiple_of(there * 16, 16), 16)],
                        dst_ref=col_recv.at[pl.ds(pl.multiple_of(w * 16, 16), 16)],
                        send_sem=col_ssem,
                        recv_sem=col_rsem,
                        device_id={"layer": g, "uvrow": there},
                        device_id_type=MESH,
                    ).start()

    mine = pl.ds(pl.multiple_of(w * 16, 16), 16)
    col_recv[mine, :] = col_send[mine, :]
    others = col_recv.at[pl.ds(0, (BANDS - 1) * 16)]
    pltpu.make_async_copy(others, others, col_rsem).wait()

    def term(k):
        held = jnp.concatenate(
            [col_recv[pl.ds(k, 64, stride=16), :], col_recv[pl.ds(8 + k, 64, stride=16), :]], axis=1
        )
        hh, hl = halves(held)
        both = lax.dot_general(
            bands[...], jnp.concatenate([hh, hl, hh], axis=0), NN, preferred_element_type=F32
        )
        image = jnp.zeros((64, 256), F32)
        for ih in range(2):
            a, b = both[:64, 128 * ih : 128 * ih + 128], both[64:, 128 * ih : 128 * ih + 128]
            turned = jnp.concatenate(
                [a * turn[0] - b * turn[1], a * turn[1] + b * turn[0]], axis=1
            )
            th, tl = halves(turned)
            image = image + lax.dot_general(
                jnp.concatenate([th, tl, th], axis=1), final[ih], NN, preferred_element_type=F32
            )
        return image[:, :128] * screen[k, 0] - image[:, 128:] * screen[k, 1]

    def red_copy(there):
        return pltpu.make_async_remote_copy(
            src_ref=red_send.at[there],
            dst_ref=red_recv.at[g],
            send_sem=red_ssem,
            recv_sem=red_rsem,
            device_id={"layer": there, "uvrow": w},
            device_id_type=MESH,
        )

    @pl.loop(1, LAYERS)
    def _(i):
        there = g ^ i
        red_send[there] = term(there)
        red_copy(there).start()

    red_recv[g] = term(g)
    others = red_recv.at[pl.ds(0, LAYERS - 1)]
    pltpu.make_async_copy(others, others, red_rsem).wait()
    total = red_recv[0]
    for layer in range(1, LAYERS):
        total = total + red_recv[layer]
    out[...] = jnp.transpose(total)

    sent = vis_send.at[pl.ds(0, (BANDS - 1) * 8)]
    pltpu.make_async_copy(sent, sent, vis_ssem).wait()
    sent = col_send.at[pl.ds(0, (BANDS - 1) * 16)]
    pltpu.make_async_copy(sent, sent, col_ssem).wait()
    sent = red_send.at[pl.ds(0, LAYERS - 1)]
    pltpu.make_async_copy(sent, sent, red_ssem).wait()


def per_device(vis_values, vis_cell, vis_offset, block_tile, block_band, layer_w):
    tables = [jnp.asarray(t) for t in host_tables()]
    vmem = pl.BlockSpec(memory_space=pltpu.VMEM)
    smem = pl.BlockSpec(memory_space=pltpu.SMEM)
    dma = pltpu.SemaphoreType.DMA
    image = pl.pallas_call(
        kernel,
        out_shape=jax.ShapeDtypeStruct((128, 64), F32),
        in_specs=[vmem] * 5 + [smem] + [vmem] * 5,
        out_specs=vmem,
        scratch_shapes=[
            pltpu.VMEM((BANDS * 8, 128), F32),
            pltpu.VMEM((BANDS * 8, 128), F32),
            pltpu.VMEM((128 * 2 * EXT, 128), F32),
            pltpu.VMEM((128, 128), F32),
            pltpu.VMEM((2, EXT * 16, 128), F32),
            pltpu.VMEM((2, (EXT - ROWS) * 16, 128), F32),
            pltpu.VMEM((BANDS * 16, 128), F32),
            pltpu.VMEM((BANDS * 16, 128), F32),
            pltpu.VMEM((LAYERS, 2, 64, 128), F32),
            pltpu.VMEM((LAYERS, 64, 128), F32),
            pltpu.VMEM((LAYERS, 64, 128), F32),
            dma, dma((BANDS,)), dma, dma, dma, dma, dma, dma,
        ],
        compiler_params=pltpu.CompilerParams(
            collective_id=0, has_side_effects=True, vmem_limit_bytes=40 * 1024 * 1024
        ),
    )(vis_values, vis_cell, vis_offset, block_tile, block_band, layer_w, *tables)
    return image.reshape(4, N)


def solution(mesh):
    placed = (
        P(("layer", "uvrow"), None, None),
        P(("layer", "uvrow"), None),
        P(("layer", "uvrow"), None),
        P(("layer", "uvrow"), None),
        P(("layer", "uvrow"), None),
        P(),
    )
    return jax.shard_map(
        per_device,
        mesh=mesh,
        in_specs=placed,
        out_specs=P(("layer", "uvrow"), None),
        check_vma=False,
    )
```

time: 270 us -> 96.5 us (0.36); the launches traced: 267 us -> 96 us
  waiting for transfers between devices: 128 us -> 0 us
  Pallas kernels: 0 us -> 87.9 us
  starting transfers between devices: 47.1 us -> 0 us
  matrix products: 43.2 us -> 0 us
  between operations: 14.4 us -> 0.03 us
  other arithmetic: 13.4 us -> 0 us
  local copies, waits for them, and re-layouts: 20 us -> 8.12 us
    pallas_call x0 -> x1, Pallas kernels: none -> 87.9 us  [per_device(): pl.pallas_call(kernel, out_shape=jax.ShapeDtypeStruct((128, 64), F32), in...]
    psum x1 -> x0, waiting for transfers between devices: 70.5 us -> none  [per_device(): summed = lax.psum(layer_term, 'layer')]
    all_to_all x4 -> x0, waiting for transfers between devices: 56.3 us -> none  [the longest x1 26.5 us: per_device(): lax.all_to_all(spectrum, 'uvrow', split_axis=2, concat_axis=4, tiled=True)]
    dot_general x24 -> x0, matrix products: 43.2 us -> none  [the longest x4 17.8 us: add_group(): jnp.einsum('nyl,nlw->nyw', weight_applied_values, column_kernel_taps, pre...]
    all_to_all x4 -> x0, starting transfers between devices: 42.5 us -> none  [the longest x1 18 us: per_device(): lax.all_to_all(send_tiles.reshape(band_count, capacity), 'uvrow', split_a...]
    scatter x2 -> x0, local copies, waits for them, and re-layouts: 5.15 us -> none  [the longest x1 4.38 us: per_device(): jnp.zeros((slot_count, 2, block_share), jnp.float32).at[position]]
    mul x7 -> x0, other arithmetic: 4.51 us -> none  [the longest x1 3.19 us: per_device(): (images[0, :, 0] * jnp.cos(phases) - images[1, :, 0] * jnp.sin(phases)) *...]
    ppermute x1 -> x0, starting transfers between devices: 4.33 us -> none  [shifted(): lax.ppermute(shard, axis, [(i, (i + by) % peers) for i in range(peers)])]
  transfers between devices with their start and end apart: 6 -> 0, of which waited for: 6 -> 0; matrix products, arithmetic and copies ran while one was open for 3% -> 0% of each run, Pallas kernels for 0% -> 0%
where the time goes in v1:
time: 96.5 us; the launch traced here: 96 us
  Pallas kernels  87.9 us (91%)
  local copies, waits for them, and re-layouts  8.12 us (8%)
    pallas_call x1, Pallas kernels, per_device(): pl.pallas_call(kernel, out_shape=jax.ShapeDtypeStruct((128, 64), F32), in...  87.9 us
    unnamed x22, local copies, waits for them, and re-layouts  7.41 us

profile of v1, /device:TPU:7, one launch (start us, length us, event | category | flops | bytes accessed | tf_op | source)
XLA Modules:
  0.0 96.0 jit_solution(9063348743059663348)
XLA Ops:
  0.0 0.0 copy-start.9
  0.0 0.0 copy-start.2
  0.0 0.8 copy.14.tile
  0.8 0.0 copy-done.9
  0.8 0.0 copy-start.8
  0.8 0.1 copy.15.band
  0.9 0.0 copy-done.2
  0.9 0.6 copy-done.8
  1.4 0.0 copy-start
  1.4 1.1 %copy-done = bf16[2,768,256]{2,1,0:T(8,128)(2,1)S(1)} copy-done((bf16[2,768,256]{2,1,0:T(8,128)(2,1)S(1)}, bf16[2,768,256]{2,1,0:T(8,128)(2,1)}, u32[]{:S(2)}) %copy-start) | copy-done | bytes 786456
  2.6 0.0 copy-start.1
  2.6 0.9 copy-done.1
  3.5 0.0 copy-start.3
  3.5 0.8 copy-done.3
  4.3 0.0 copy-start.4
  4.4 0.8 copy-done.4
  5.2 0.0 copy-start.5
  5.2 0.8 copy-done.5
  5.9 0.0 copy-start.6
  5.9 0.8 copy-done.6
  6.7 0.0 copy-start.7
  6.7 0.7 copy-done.7
  7.4 87.9 %shard_map.109 = f32[128,64]{1,0:T(8,128)S(1)} custom-call(f32[64,2,128]{2,1,0:T(2,128)S(1)} %copy-done.2, s32[64,128]{1,0:T(8,128)S(1)} %copy-done.5, s32[64,128]{1,0:T(8,128)S(1)} %copy-done.6, s32[64,1]{1,0:T(8,128)S(1)} %copy.14.tile, s32[64,1]{1,0:T(8,128)S(1)} %copy.15.band, f32[8]{0:T(128)S(1)} %copy-done.8, bf16[128,768]{1,0:T(8,128)(2,1)S(1)} %copy-done.1, ...), custom_call_target="tpu_custom_call" | custom-call | tf_op jit(solution)/shard_map/pallas_call | solution.py:349
  95.3 0.7 reshape.3
Async XLA Ops:
  0.0 0.8 copy-start.9
  0.0 0.9 copy-start.2
  0.8 0.7 copy-start.8
  1.4 1.1 %copy-start = (bf16[2,768,256]{2,1,0:T(8,128)(2,1)S(1)}, bf16[2,768,256]{2,1,0:T(8,128)(2,1)}, u32[]{:S(2)}) copy-start(bf16[2,768,256]{2,1,0:T(8,128)(2,1)} %constant.14.clone.final) | copy-start | bytes 2359300
  2.6 0.9 copy-start.1
  3.5 0.8 copy-start.3
  4.3 0.8 copy-start.4
  5.2 0.8 copy-start.5
  5.9 0.8 copy-start.6
  6.7 0.7 copy-start.7

commit v2 on v1

--- a/solution.py
+++ b/solution.py
@@ -21,6 +21,10 @@
 EXT = 40
 SIGMA = 1.45
 WIDTH = 0.6
+CHUNKS = 2
+SLOTS = 2 * BANDS // CHUNKS
+GROUP = 8
+ROW_GROUP = 8
 TAP_SCALE = math.sqrt(math.log2(math.e) / (2.0 * SIGMA * SIGMA))
 MESH = pl.DeviceIdType.MESH
 F32 = jnp.float32
@@ -28,18 +32,15 @@
 NN = (((1,), (0,)), ((), ()))
 NT = (((1,), (1,)), ((), ()))
 
-
 def halves(x):
     high = x.astype(BF16)
     low = (x - high.astype(F32)).astype(BF16)
     return high, low
 
-
 def host_halves(x):
     high = x.astype(np.float32).astype(ml_dtypes.bfloat16)
     low = (x - high.astype(np.float64)).astype(np.float32).astype(ml_dtypes.bfloat16)
     return high, low
-
 
 def host_tables():
     p1 = np.array([16 * k + z for z in range(16) for k in range(8)])
@@ -73,7 +74,6 @@
     final = np.concatenate([high, high, low], axis=1)
     return outer, twist, bands, turn, final
 
-
 def cos_sin_turns(turns):
     quarters = turns * 4.0
     whole = jnp.round(quarters)
@@ -89,21 +89,32 @@
     b = jnp.where((n & 2) == 2, -b, b)
     return a, b
 
-
 def wrapped(pixel):
     return (((pixel + N // 2) & (N - 1)) - N // 2).astype(F32) * (WIDTH / N)
 
-
 def kernel(
-    values, cell, offset, tile, band, depth_ref,
-    outer, twist, bands, turn, final, out,
+    values_hbm, cell_hbm, offset_hbm, tile_hbm, band_hbm, depth_hbm,
+    outer_hbm, twist_hbm, bands_hbm, turn_hbm, final_hbm, out,
+    values, cell, offset, tile, band, depth_ref, outer, twist, bands, turn, final,
     vis_send, vis_recv, parts, tiles, spec, spill, col_send, col_recv, screen, red_send, red_recv,
-    vis_ssem, vis_rsem, spill_ssem, spill_rsem, col_ssem, col_rsem, red_ssem, red_rsem,
+    load_sem, vis_ssem, vis_rsem, spill_ssem, spill_rsem, col_ssem, col_rsem, red_ssem, red_rsem,
 ):
     g, w = lax.axis_index("layer"), lax.axis_index("uvrow")
     z, x = w >> 2, w & 3
 
     barrier = pltpu.get_barrier_semaphore()
+    loads = [
+        pltpu.make_async_copy(there, here, load_sem.at[n])
+        for n, (there, here) in enumerate(
+            [
+                (band_hbm, band), (tile_hbm, tile), (cell_hbm, cell), (offset_hbm, offset),
+                (values_hbm, values), (depth_hbm, depth_ref), (twist_hbm, twist), (outer_hbm, outer),
+                (bands_hbm, bands), (turn_hbm, turn), (final_hbm, final),
+            ]
+        )
+    ]
+    for load in loads:
+        load.start()
 
     @pl.loop(1, BANDS)
     def _(i):
@@ -113,10 +124,14 @@
     def _(i):
         pl.semaphore_signal(barrier, inc=1, device_id={"layer": g ^ i, "uvrow": w}, device_id_type=MESH)
 
+    for load in loads[:6]:
+        load.wait()
+
     row_id = lax.broadcasted_iota(jnp.int32, (BLOCKS, BLOCKS), 0)
     col_id = lax.broadcasted_iota(jnp.int32, (BLOCKS, BLOCKS), 1)
-    own = jnp.broadcast_to(band[...], (BLOCKS, BLOCKS))
-    other = jnp.sum(jnp.where(row_id == col_id, own, 0), axis=0, keepdims=True)
+    other = jnp.broadcast_to(band[...], (BLOCKS, BLOCKS))
+    own = jnp.sum(jnp.where(row_id == col_id, other, 0), axis=1, keepdims=True)
+    tile_of = jnp.sum(jnp.where(row_id == col_id, jnp.broadcast_to(tile[...], (BLOCKS, BLOCKS)), 0), axis=1, keepdims=True)
     same = own == other
     rank = jnp.sum(jnp.where(same & (row_id < col_id), 1, 0), axis=0, keepdims=True)
     cells = cell[...].astype(F32)
@@ -124,7 +139,7 @@
     cols = cells - rows * SPAN
     shifts = offset[...]
     u_place = rows * 8.0 + (shifts >> 3).astype(F32)
-    v_place = (cols + tile[...].astype(F32) * TW) * 8.0 + (shifts & 7).astype(F32)
+    v_place = (cols + tile_of.astype(F32) * TW) * 8.0 + (shifts & 7).astype(F32)
     data = jnp.concatenate([values[:, 0, :], values[:, 1, :], u_place, v_place], axis=1)
     first = data.astype(BF16)
     rest = data - first.astype(F32)
@@ -169,7 +184,9 @@
         vis_copy(i).start()
 
     mine = pl.ds(pl.multiple_of(w * 8, 8), 8)
-    vis_recv[mine, :] = vis_send[mine, :]
+    pltpu.make_async_copy(vis_send.at[mine], vis_recv.at[mine], vis_rsem.at[0]).start()
+    for load in loads[6:]:
+        load.wait()
 
     row_axis = lax.broadcasted_iota(jnp.int32, (EXT, 128), 0).astype(F32)
     col_axis = lax.broadcasted_iota(jnp.int32, (TW, 128), 0).astype(F32)
@@ -180,44 +197,42 @@
         inside = (axis >= begin) & (axis < begin + K)
         return jnp.where(inside, jnp.exp2(-(far * far)), 0.0)
 
-    @pl.loop(0, BANDS)
-    def _(i):
-        there = pl.multiple_of((w ^ i) * 8, 8)
-
-        @pl.when(i > 0)
-        def _():
-            piece = vis_recv.at[pl.ds(there, 8)]
-            pltpu.make_async_copy(piece, piece, vis_rsem.at[i]).wait()
-
-        message = vis_recv[pl.ds(there, 8), :]
-        for j in range(2):
-            v_all = message[4 * j + 3 : 4 * j + 4]
-            number = jnp.floor(v_all * (1.0 / 1024))
-            row_taps = taps(row_axis, message[4 * j + 2 : 4 * j + 3])
-            weighted = jnp.concatenate(
-                [row_taps * message[4 * j : 4 * j + 1], row_taps * message[4 * j + 1 : 4 * j + 2]], axis=0
-            )
-            col_taps = taps(col_axis, v_all - number * 1024.0)
-            wh, wl = halves(weighted)
-            ch, cl = halves(col_taps)
-            patch = lax.dot_general(
-                jnp.concatenate([wh, wl, wh], axis=1),
-                jnp.concatenate([ch, ch, cl], axis=1),
-                NT,
-                preferred_element_type=F32,
-            )
-            parts[pl.ds(pl.multiple_of((2 * i + j) * 2 * EXT, 16), 2 * EXT), :] = patch
-            tiles[pl.ds(2 * i + j, 1), :] = number
-
-    by_slot = jnp.transpose(tiles[...])[:16]
-    p0 = lax.broadcasted_iota(jnp.int32, (16, 128), 0).astype(F32)
-    cos, sin = cos_sin_turns(by_slot * p0 * (1.0 / 16))
-    mh, ml = halves(jnp.concatenate([cos, sin], axis=0))
-    mix = jnp.concatenate([mh, mh, ml], axis=1)
-
-    def tile_row(u):
-        re = parts[pl.ds(u, 128, stride=2 * EXT), :]
-        im = parts[pl.ds(u + EXT, 128, stride=2 * EXT), :]
+    def patches(i, count):
+        messages = []
+        for n in range(count):
+            piece = vis_recv.at[pl.ds(pl.multiple_of((w ^ (i + n)) * 8, 8), 8)]
+            pltpu.make_async_copy(piece, piece, vis_rsem.at[i + n]).wait()
+        for n in range(count):
+            messages.append(vis_recv[pl.ds(pl.multiple_of((w ^ (i + n)) * 8, 8), 8), :])
+        for n in range(count):
+            message = messages[n]
+            for j in range(2):
+                slot = (2 * (i + n) + j) & (SLOTS - 1)
+                v_all = message[4 * j + 3 : 4 * j + 4]
+                number = jnp.floor(v_all * (1.0 / 1024))
+                row_taps = taps(row_axis, message[4 * j + 2 : 4 * j + 3])
+                weighted = jnp.concatenate(
+                    [row_taps * message[4 * j : 4 * j + 1], row_taps * message[4 * j + 1 : 4 * j + 2]], axis=0
+                )
+                col_taps = taps(col_axis, v_all - number * 1024.0)
+                wh, wl = halves(weighted)
+                ch, cl = halves(col_taps)
+                patch = lax.dot_general(
+                    jnp.concatenate([wh, wl, wh], axis=1),
+                    jnp.concatenate([ch, ch, cl], axis=1),
+                    NT,
+                    preferred_element_type=F32,
+                )
+                parts[pl.ds(pl.multiple_of(slot * 2 * EXT, 16), 2 * EXT), :] = patch
+                for copy in range(3):
+                    tiles[pl.ds(copy * SLOTS + slot, 1), :] = number
+
+    p0 = lax.broadcasted_iota(jnp.int32, (16, 3 * SLOTS), 0).astype(F32)
+    exact = lax.broadcasted_iota(jnp.int32, (32, 3 * SLOTS), 1) < 2 * SLOTS
+
+    def tile_row(u, mix, begin):
+        re = parts[pl.ds(u, SLOTS, stride=2 * EXT), :]
+        im = parts[pl.ds(u + EXT, SLOTS, stride=2 * EXT), :]
         ph, plo = halves(jnp.concatenate([re, im], axis=1))
         both = lax.dot_general(
             mix, jnp.concatenate([ph, plo, ph], axis=0), NN, preferred_element_type=F32
@@ -226,14 +241,15 @@
         im = both[:16, 128:] + both[16:, :128]
         tc, ts = twist[0], twist[1]
         at = pl.ds(pl.multiple_of(u * 16, 16), 16)
-        spec[0, at, :] = re * tc - im * ts
-        spec[1, at, :] = re * ts + im * tc
-
-    @pl.loop(ROWS, EXT)
-    def _(u):
-        tile_row(u)
-
-    after, before = (w + 1) & (BANDS - 1), (w + BANDS - 1) & (BANDS - 1)
+        new_re, new_im = re * tc - im * ts, re * ts + im * tc
+        if begin:
+            spec[0, at, :] = new_re
+            spec[1, at, :] = new_im
+        else:
+            spec[0, at, :] += new_re
+            spec[1, at, :] += new_im
+
+    after = (w + 1) & (BANDS - 1)
     spill_copy = pltpu.make_async_remote_copy(
         src_ref=spec.at[:, pl.ds(ROWS * 16, (EXT - ROWS) * 16)],
         dst_ref=spill,
@@ -242,11 +258,30 @@
         device_id={"layer": g, "uvrow": after},
         device_id_type=MESH,
     )
-    spill_copy.start()
-
-    @pl.loop(0, ROWS)
-    def _(u):
-        tile_row(u)
+    for chunk in range(CHUNKS):
+        start = chunk * (SLOTS // 2)
+
+        @pl.loop(start, start + SLOTS // 2, step=GROUP)
+        def _(i):
+            patches(i, GROUP)
+
+        by_slot = jnp.transpose(tiles[...])[:16, : 3 * SLOTS]
+        cos, sin = cos_sin_turns(by_slot * p0 * (1.0 / 16))
+        mh, ml = halves(jnp.concatenate([cos, sin], axis=0))
+        mix = jnp.where(exact, mh, ml)
+
+        @pl.loop(ROWS, EXT, step=ROW_GROUP)
+        def _(u):
+            for n in range(ROW_GROUP):
+                tile_row(u + n, mix, chunk == 0)
+
+        if chunk == CHUNKS - 1:
+            spill_copy.start()
+
+        @pl.loop(0, ROWS, step=ROW_GROUP)
+        def _(u):
+            for n in range(ROW_GROUP):
+                tile_row(u + n, mix, chunk == 0)
 
     spill_copy.wait()
     over = pl.ds(0, (EXT - ROWS) * 16)
@@ -340,22 +375,26 @@
     sent = red_send.at[pl.ds(0, LAYERS - 1)]
     pltpu.make_async_copy(sent, sent, red_ssem).wait()
 
-
 def per_device(vis_values, vis_cell, vis_offset, block_tile, block_band, layer_w):
     tables = [jnp.asarray(t) for t in host_tables()]
+    operands = [
+        vis_values, vis_cell, vis_offset, block_tile.reshape(1, BLOCKS), block_band.reshape(1, BLOCKS), layer_w, *tables,
+    ]
+    hbm = pl.BlockSpec(memory_space=pltpu.HBM)
     vmem = pl.BlockSpec(memory_space=pltpu.VMEM)
-    smem = pl.BlockSpec(memory_space=pltpu.SMEM)
     dma = pltpu.SemaphoreType.DMA
+    held = [(pltpu.SMEM if a is layer_w else pltpu.VMEM)(a.shape, a.dtype) for a in operands]
     image = pl.pallas_call(
         kernel,
         out_shape=jax.ShapeDtypeStruct((128, 64), F32),
-        in_specs=[vmem] * 5 + [smem] + [vmem] * 5,
+        in_specs=[hbm] * len(operands),
         out_specs=vmem,
         scratch_shapes=[
+            *held,
             pltpu.VMEM((BANDS * 8, 128), F32),
             pltpu.VMEM((BANDS * 8, 128), F32),
-            pltpu.VMEM((128 * 2 * EXT, 128), F32),
-            pltpu.VMEM((128, 128), F32),
+            pltpu.VMEM((SLOTS * 2 * EXT, 128), F32),
+            pltpu.VMEM((max(128, 3 * SLOTS), 128), F32),
             pltpu.VMEM((2, EXT * 16, 128), F32),
             pltpu.VMEM((2, (EXT - ROWS) * 16, 128), F32),
             pltpu.VMEM((BANDS * 16, 128), F32),
@@ -363,14 +402,13 @@
             pltpu.VMEM((LAYERS, 2, 64, 128), F32),
             pltpu.VMEM((LAYERS, 64, 128), F32),
             pltpu.VMEM((LAYERS, 64, 128), F32),
-            dma, dma((BANDS,)), dma, dma, dma, dma, dma, dma,
+            dma((len(operands),)), dma, dma((BANDS,)), dma, dma, dma, dma, dma, dma,
         ],
         compiler_params=pltpu.CompilerParams(
-            collective_id=0, has_side_effects=True, vmem_limit_bytes=40 * 1024 * 1024
+            collective_id=0, has_side_effects=True, vmem_limit_bytes=60 * 1024 * 1024
         ),
-    )(vis_values, vis_cell, vis_offset, block_tile, block_band, layer_w, *tables)
+    )(*operands)
     return image.reshape(4, N)
-
 
 def solution(mesh):
     placed = (

time: 96.5 us -> 82.9 us (0.86)
  Pallas kernels: 87.9 us -> 81.1 us
  local copies, waits for them, and re-layouts: 8.12 us -> 1.55 us
    unnamed x22 -> x0, local copies, waits for them, and re-layouts: 7.41 us -> none
    pallas_call x1, Pallas kernels: 87.9 us -> 81.1 us  [per_device(): pl.pallas_call(kernel, out_shape=jax.ShapeDtypeStruct((128, 64), F32), in...]
where the time goes in v2:
time: 82.9 us; the launch traced here: 82.7 us
  Pallas kernels  81.1 us (98%)
  local copies, waits for them, and re-layouts  1.55 us (2%)
    pallas_call x1, Pallas kernels, per_device(): pl.pallas_call(kernel, out_shape=jax.ShapeDtypeStruct((128, 64), F32), in...  81.1 us

profile of v2, /device:TPU:7, one launch (start us, length us, event | category | flops | bytes accessed | tf_op | source)
XLA Modules:
  0.0 82.7 jit_solution(1966577045173563351)
XLA Ops:
  0.0 81.1 %shard_map.109 = f32[128,64]{1,0:T(8,128)} custom-call(f32[64,2,128]{2,1,0:T(2,128)} %values_hbm.1, s32[64,128]{1,0:T(8,128)} %cell_hbm.1, s32[64,128]{1,0:T(8,128)} %offset_hbm.1, s32[1,64]{1,0:T(1,128)} %bitcast.2, s32[1,64]{1,0:T(1,128)} %bitcast.3, f32[8]{0:T(128)} %depth_hbm.1, bf16[128,768]{1,0:T(8,128)(2,1)} %constant.10.clone.outer_hbm, ...), custom_call_target="tpu_custom_call" | custom-call | tf_op jit(solution)/shard_map/pallas_call | solution.py:387
  81.2 1.5 %reshape.11 = f32[4,2048]{1,0:T(4,128)} reshape(f32[128,64]{1,0:T(8,128)} %shard_map.109) | data formatting | bytes 65536 | tf_op jit(solution)/shard_map/reshape | solution.py:411

commit v3 on v2

--- a/solution.py
+++ b/solution.py
@@ -13,6 +13,7 @@
 N = 2048
 TW = 128
 K = 8
+OVS = 8
 SPAN = TW - K + 1
 BANDS = 64
 LAYERS = 8
@@ -25,12 +26,19 @@
 SLOTS = 2 * BANDS // CHUNKS
 GROUP = 8
 ROW_GROUP = 8
+LATE = 8
 TAP_SCALE = math.sqrt(math.log2(math.e) / (2.0 * SIGMA * SIGMA))
 MESH = pl.DeviceIdType.MESH
 F32 = jnp.float32
 BF16 = jnp.bfloat16
 NN = (((1,), (0,)), ((), ()))
 NT = (((1,), (1,)), ((), ()))
+
+def tier_of(w):
+    return jnp.where((w & 3) == 0, 1 + (w >> 5), 0)
+
+def far_first(n, count):
+    return count // 2 + ((n + 1) >> 1) * (1 - 2 * (n & 1))
 
 def halves(x):
     high = x.astype(BF16)
@@ -96,7 +104,7 @@
     values_hbm, cell_hbm, offset_hbm, tile_hbm, band_hbm, depth_hbm,
     outer_hbm, twist_hbm, bands_hbm, turn_hbm, final_hbm, out,
     values, cell, offset, tile, band, depth_ref, outer, twist, bands, turn, final,
-    vis_send, vis_recv, parts, tiles, spec, spill, col_send, col_recv, screen, red_send, red_recv,
+    vis_send, vis_recv, parts, tiles, spec, spill, col_send, col_recv, partial, screen, red_send, red_recv, lines, pairs, ready,
     load_sem, vis_ssem, vis_rsem, spill_ssem, spill_rsem, col_ssem, col_rsem, red_ssem, red_rsem,
 ):
     g, w = lax.axis_index("layer"), lax.axis_index("uvrow")
@@ -116,9 +124,15 @@
     for load in loads:
         load.start()
 
-    @pl.loop(1, BANDS)
-    def _(i):
-        pl.semaphore_signal(barrier, inc=1, device_id={"layer": g, "uvrow": w ^ i}, device_id_type=MESH)
+    tier = tier_of(w)
+
+    @pl.loop(0, BANDS - 1)
+    def _(n):
+        there = (w + far_first(n, BANDS)) & (BANDS - 1)
+
+        @pl.when(tier_of(there) >= tier)
+        def _():
+            pl.semaphore_signal(barrier, inc=1, device_id={"layer": g, "uvrow": there}, device_id_type=MESH)
 
     @pl.loop(1, LAYERS)
     def _(i):
@@ -166,66 +180,114 @@
         screen[k, 0] = cos * (1.0 / N)
         screen[k, 1] = sin * (1.0 / N)
 
-    pl.semaphore_wait(barrier, BANDS - 1 + LAYERS - 1)
-
-    def vis_copy(i):
-        there = w ^ i
+    pl.semaphore_wait(barrier, BANDS - 2 * LATE - 1 + LATE * tier + LAYERS - 1)
+
+    @pl.when(tier > 0)
+    def _():
+        @pl.loop(0, BANDS - 1)
+        def _(n):
+            there = (w + far_first(n, BANDS)) & (BANDS - 1)
+
+            @pl.when(tier_of(there) < tier)
+            def _():
+                pl.semaphore_signal(
+                    ready.at[tier - 1], inc=1, device_id={"layer": g, "uvrow": there}, device_id_type=MESH
+                )
+
+    def vis_copy(there):
         return pltpu.make_async_remote_copy(
             src_ref=vis_send.at[pl.ds(pl.multiple_of(there * 8, 8), 8)],
             dst_ref=vis_recv.at[pl.ds(pl.multiple_of(w * 8, 8), 8)],
             send_sem=vis_ssem,
-            recv_sem=vis_rsem.at[i],
+            recv_sem=vis_rsem.at[w],
             device_id={"layer": g, "uvrow": there},
             device_id_type=MESH,
         )
 
-    @pl.loop(1, BANDS)
-    def _(i):
-        vis_copy(i).start()
+    @pl.loop(0, BANDS - 1)
+    def _(n):
+        there = (w + far_first(n, BANDS)) & (BANDS - 1)
+
+        @pl.when(tier_of(there) <= tier)
+        def _():
+            vis_copy(there).start()
+
+    for later in range(2):
+
+        @pl.when(tier <= later)
+        def _():
+            pl.semaphore_wait(ready.at[later], LATE)
+
+            @pl.loop(0, LATE)
+            def _(n):
+                vis_copy(4 * (LATE * later + ((n + z) & (LATE - 1)))).start()
 
     mine = pl.ds(pl.multiple_of(w * 8, 8), 8)
-    pltpu.make_async_copy(vis_send.at[mine], vis_recv.at[mine], vis_rsem.at[0]).start()
+    pltpu.make_async_copy(vis_send.at[mine], vis_recv.at[mine], vis_rsem.at[w]).start()
     for load in loads[6:]:
         load.wait()
 
-    row_axis = lax.broadcasted_iota(jnp.int32, (EXT, 128), 0).astype(F32)
-    col_axis = lax.broadcasted_iota(jnp.int32, (TW, 128), 0).astype(F32)
-
-    def taps(axis, place):
-        begin = jnp.floor(place * 0.125)
-        far = axis * TAP_SCALE - (place * 0.125 + (K - 1) / 2.0) * TAP_SCALE
-        inside = (axis >= begin) & (axis < begin + K)
-        return jnp.where(inside, jnp.exp2(-(far * far)), 0.0)
+    sublane = lax.broadcasted_iota(jnp.int32, (8, 128), 0)
+
+    def source(n):
+        block = n >> 4
+        early = 4 * ((z + n) & 15) + 1 + lax.rem(x + block, 3)
+        late = 4 * ((n & 8) + ((z + n) & 7))
+        return jnp.where(block == 3, late, early)
+
+    def taps(place):
+        cell = place >> 3
+        tap = (sublane - cell) & 7
+        group = (cell + tap - sublane) >> 3
+        far = (tap.astype(F32) - ((place & 7).astype(F32) * (1.0 / OVS) + (K - 1) / 2.0)) * TAP_SCALE
+        return group, jnp.exp2(-(far * far))
+
+    def spread(group, value, count):
+        return jnp.concatenate([jnp.where(group == m, value, 0.0) for m in range(count)], axis=0)
+
+    def split(value):
+        high = value.astype(BF16).astype(F32)
+        return high, value - high
 
     def patches(i, count):
-        messages = []
+        begins = [pl.multiple_of(source(i + n) * 8, 8) for n in range(count)]
         for n in range(count):
-            piece = vis_recv.at[pl.ds(pl.multiple_of((w ^ (i + n)) * 8, 8), 8)]
-            pltpu.make_async_copy(piece, piece, vis_rsem.at[i + n]).wait()
+            piece = vis_recv.at[pl.ds(begins[n], 8)]
+            pltpu.make_async_copy(piece, piece, vis_rsem.at[source(i + n)]).wait()
         for n in range(count):
-            messages.append(vis_recv[pl.ds(pl.multiple_of((w ^ (i + n)) * 8, 8), 8), :])
-        for n in range(count):
-            message = messages[n]
+            message = vis_recv[pl.ds(begins[n], 8), :]
+            rows_high, rows_low, cols_high, cols_low = [], [], [], []
             for j in range(2):
                 slot = (2 * (i + n) + j) & (SLOTS - 1)
-                v_all = message[4 * j + 3 : 4 * j + 4]
-                number = jnp.floor(v_all * (1.0 / 1024))
-                row_taps = taps(row_axis, message[4 * j + 2 : 4 * j + 3])
-                weighted = jnp.concatenate(
-                    [row_taps * message[4 * j : 4 * j + 1], row_taps * message[4 * j + 1 : 4 * j + 2]], axis=0
-                )
-                col_taps = taps(col_axis, v_all - number * 1024.0)
-                wh, wl = halves(weighted)
-                ch, cl = halves(col_taps)
-                patch = lax.dot_general(
-                    jnp.concatenate([wh, wl, wh], axis=1),
-                    jnp.concatenate([ch, ch, cl], axis=1),
-                    NT,
-                    preferred_element_type=F32,
-                )
-                parts[pl.ds(pl.multiple_of(slot * 2 * EXT, 16), 2 * EXT), :] = patch
+                u_place = message[4 * j + 2 : 4 * j + 3].astype(jnp.int32)
+                v_place = message[4 * j + 3 : 4 * j + 4].astype(jnp.int32)
+                row_group, row_taps = taps(u_place)
+                col_group, col_taps = taps(v_place & (TW * OVS - 1))
+                re = split(row_taps * message[4 * j : 4 * j + 1])
+                im = split(row_taps * message[4 * j + 1 : 4 * j + 2])
+                cols = split(col_taps)
+                wh, wl = [
+                    jnp.concatenate(
+                        [spread(row_group, re[p], EXT // 8), spread(row_group, im[p], EXT // 8)], axis=0
+                    ).astype(BF16)
+                    for p in range(2)
+                ]
+                ch, cl = [spread(col_group, cols[p], TW // 8).astype(BF16) for p in range(2)]
+                rows_high.append(wh)
+                rows_low.append(wl)
+                cols_high.append(ch)
+                cols_low.append(cl)
+                number = (v_place >> 10).astype(F32)
                 for copy in range(3):
                     tiles[pl.ds(copy * SLOTS + slot, 1), :] = number
+            none = jnp.zeros((2 * EXT, 128), BF16)
+            first = [jnp.concatenate([rows_high[0], none], axis=1), jnp.concatenate([none, rows_high[1]], axis=1)]
+            low = lax.dot_general(
+                jnp.concatenate(first, axis=0), jnp.concatenate(cols_low, axis=1), NT, preferred_element_type=F32
+            )
+            high = [lax.dot_general(jnp.concatenate([rows_high[j], rows_low[j]], axis=1), jnp.concatenate([cols_high[j], cols_high[j]], axis=1), NT, preferred_element_type=F32) for j in range(2)]
+            patch = jnp.concatenate(high, axis=0) + low
+            parts[pl.ds(pl.multiple_of(((2 * (i + n)) & (SLOTS - 1)) * 2 * EXT, 16), 4 * EXT), :] = patch
 
     p0 = lax.broadcasted_iota(jnp.int32, (16, 3 * SLOTS), 0).astype(F32)
     exact = lax.broadcasted_iota(jnp.int32, (32, 3 * SLOTS), 1) < 2 * SLOTS
@@ -287,62 +349,65 @@
     over = pl.ds(0, (EXT - ROWS) * 16)
     spec[:, over, :] = spec[:, over, :] + spill[...]
 
-    for pair in range(8):
-        there_x, ih = pair // 2, pair % 2
-        operand = []
-        for il in range(2):
-            re = spec[0, pl.ds(2 * pair + il, ROWS, stride=16), :]
-            im = spec[1, pl.ds(2 * pair + il, ROWS, stride=16), :]
-            operand.append(jnp.concatenate([re, -im], axis=1))
-            operand.append(jnp.concatenate([im, re], axis=1))
-        oh, ol = halves(jnp.concatenate(operand, axis=0))
-        half = lax.dot_general(
-            outer[...], jnp.concatenate([oh, ol, oh], axis=1), NT, preferred_element_type=F32
-        )
-        for there_z in range(16):
-            at = (4 * there_z + there_x) * 16 + 8 * ih
-            col_send[at : at + 8, :] = half[8 * there_z : 8 * there_z + 8]
-        if ih == 1:
-
-            @pl.loop(0, 16)
-            def _(dz):
-                there = ((z ^ dz) << 2) + there_x
-
-                @pl.when(there != w)
-                def _():
-                    pltpu.make_async_remote_copy(
-                        src_ref=col_send.at[pl.ds(pl.multiple_of(there * 16, 16), 16)],
-                        dst_ref=col_recv.at[pl.ds(pl.multiple_of(w * 16, 16), 16)],
-                        send_sem=col_ssem,
-                        recv_sem=col_rsem,
-                        device_id={"layer": g, "uvrow": there},
-                        device_id_type=MESH,
-                    ).start()
-
-    mine = pl.ds(pl.multiple_of(w * 16, 16), 16)
-    col_recv[mine, :] = col_send[mine, :]
-    others = col_recv.at[pl.ds(0, (BANDS - 1) * 16)]
-    pltpu.make_async_copy(others, others, col_rsem).wait()
-
-    def term(k):
+    for ih in range(2):
+        for dx in range(4):
+            there_x = x ^ dx
+            operand = []
+            for il in range(2):
+                place = pl.ds(4 * there_x + 2 * ih + il, ROWS, stride=16)
+                re, im = spec[0, place, :], spec[1, place, :]
+                operand.append(jnp.concatenate([re, -im], axis=1))
+                operand.append(jnp.concatenate([im, re], axis=1))
+            oh, ol = halves(jnp.concatenate(operand, axis=0))
+            half = lax.dot_general(
+                outer[...], jnp.concatenate([oh, ol, oh], axis=1), NT, preferred_element_type=F32
+            )
+            for there_z in range(16):
+                at = pl.multiple_of((4 * there_z + there_x) * 8, 8)
+                col_send[ih, pl.ds(at, 8), :] = half[8 * there_z : 8 * there_z + 8]
+
+            @pl.loop(0, 16 if dx else 15)
+            def _(n):
+                there = (((z + far_first(n, 16)) & 15) << 2) + there_x
+                pltpu.make_async_remote_copy(
+                    src_ref=col_send.at[ih, pl.ds(pl.multiple_of(there * 8, 8), 8)],
+                    dst_ref=col_recv.at[ih, pl.ds(pl.multiple_of(w * 8, 8), 8)],
+                    send_sem=col_ssem,
+                    recv_sem=col_rsem.at[ih],
+                    device_id={"layer": g, "uvrow": there},
+                    device_id_type=MESH,
+                ).start()
+
+    mine = pl.ds(pl.multiple_of(w * 8, 8), 8)
+    for ih in range(2):
+        col_recv[ih, mine, :] = col_send[ih, mine, :]
+
+    def arrived(ih):
+        others = col_recv.at[ih, pl.ds(0, (BANDS - 1) * 8)]
+        pltpu.make_async_copy(others, others, col_rsem.at[ih]).wait()
+
+    def half_image(ih, first, count):
         held = jnp.concatenate(
-            [col_recv[pl.ds(k, 64, stride=16), :], col_recv[pl.ds(8 + k, 64, stride=16), :]], axis=1
+            [col_recv[ih, pl.ds(first + k, 64, stride=8), :] for k in range(count)], axis=1
         )
         hh, hl = halves(held)
         both = lax.dot_general(
             bands[...], jnp.concatenate([hh, hl, hh], axis=0), NN, preferred_element_type=F32
         )
-        image = jnp.zeros((64, 256), F32)
-        for ih in range(2):
-            a, b = both[:64, 128 * ih : 128 * ih + 128], both[64:, 128 * ih : 128 * ih + 128]
-            turned = jnp.concatenate(
-                [a * turn[0] - b * turn[1], a * turn[1] + b * turn[0]], axis=1
+        turned = []
+        for k in range(count):
+            a, b = both[:64, 128 * k : 128 * k + 128], both[64:, 128 * k : 128 * k + 128]
+            turned.append(
+                jnp.concatenate([a * turn[0] - b * turn[1], a * turn[1] + b * turn[0]], axis=1)
             )
-            th, tl = halves(turned)
-            image = image + lax.dot_general(
-                jnp.concatenate([th, tl, th], axis=1), final[ih], NN, preferred_element_type=F32
-            )
-        return image[:, :128] * screen[k, 0] - image[:, 128:] * screen[k, 1]
+        th, tl = halves(jnp.concatenate(turned, axis=0))
+        return lax.dot_general(
+            jnp.concatenate([th, tl, th], axis=1), final[ih], NN, preferred_element_type=F32
+        )
+
+    arrived(0)
+    for first in range(0, LAYERS, 4):
+        partial[64 * first : 64 * first + 256, :] = half_image(0, first, 4)
 
     def red_copy(there):
         return pltpu.make_async_remote_copy(
@@ -354,23 +419,33 @@
             device_id_type=MESH,
         )
 
-    @pl.loop(1, LAYERS)
-    def _(i):
-        there = g ^ i
-        red_send[there] = term(there)
-        red_copy(there).start()
-
-    red_recv[g] = term(g)
+    arrived(1)
+    for step in range(2):
+        first = ((g >> 2) ^ (1 - step)) * 4
+        image = half_image(1, first, 4) + partial[pl.ds(pl.multiple_of(first * 64, 256), 256), :]
+        for n in range(4):
+            there = first + n
+            piece = image[64 * n : 64 * n + 64]
+            red_send[there] = piece[:, :128] * screen[there, 0] - piece[:, 128:] * screen[there, 1]
+
+            @pl.when(there != g)
+            def _():
+                red_copy(there).start()
+
+    red_recv[g] = red_send[g]
     others = red_recv.at[pl.ds(0, LAYERS - 1)]
     pltpu.make_async_copy(others, others, red_rsem).wait()
     total = red_recv[0]
     for layer in range(1, LAYERS):
         total = total + red_recv[layer]
-    out[...] = jnp.transpose(total)
+    lines[...] = jnp.transpose(total)
+    pairs[...] = jnp.concatenate([lines[pl.ds(n, 64, stride=2), :] for n in range(2)], axis=1)
+    for n in range(16):
+        out[:, 128 * n : 128 * n + 128] = pairs[pl.ds(n, 4, stride=16), :]
 
     sent = vis_send.at[pl.ds(0, (BANDS - 1) * 8)]
     pltpu.make_async_copy(sent, sent, vis_ssem).wait()
-    sent = col_send.at[pl.ds(0, (BANDS - 1) * 16)]
+    sent = col_send.at[:, pl.ds(0, (BANDS - 1) * 8)]
     pltpu.make_async_copy(sent, sent, col_ssem).wait()
     sent = red_send.at[pl.ds(0, LAYERS - 1)]
     pltpu.make_async_copy(sent, sent, red_ssem).wait()
@@ -384,9 +459,9 @@
     vmem = pl.BlockSpec(memory_space=pltpu.VMEM)
     dma = pltpu.SemaphoreType.DMA
     held = [(pltpu.SMEM if a is layer_w else pltpu.VMEM)(a.shape, a.dtype) for a in operands]
-    image = pl.pallas_call(
+    return pl.pallas_call(
         kernel,
-        out_shape=jax.ShapeDtypeStruct((128, 64), F32),
+        out_shape=jax.ShapeDtypeStruct((4, N), F32),
         in_specs=[hbm] * len(operands),
         out_specs=vmem,
         scratch_shapes=[
@@ -397,18 +472,21 @@
             pltpu.VMEM((max(128, 3 * SLOTS), 128), F32),
             pltpu.VMEM((2, EXT * 16, 128), F32),
             pltpu.VMEM((2, (EXT - ROWS) * 16, 128), F32),
-            pltpu.VMEM((BANDS * 16, 128), F32),
-            pltpu.VMEM((BANDS * 16, 128), F32),
+            pltpu.VMEM((2, BANDS * 8, 128), F32),
+            pltpu.VMEM((2, BANDS * 8, 128), F32),
+            pltpu.VMEM((LAYERS * 64, 256), F32),
             pltpu.VMEM((LAYERS, 2, 64, 128), F32),
             pltpu.VMEM((LAYERS, 64, 128), F32),
             pltpu.VMEM((LAYERS, 64, 128), F32),
-            dma((len(operands),)), dma, dma((BANDS,)), dma, dma, dma, dma, dma, dma,
+            pltpu.VMEM((128, 64), F32),
+            pltpu.VMEM((64, 128), F32),
+            pltpu.SemaphoreType.REGULAR((2,)),
+            dma((len(operands),)), dma, dma((BANDS,)), dma, dma, dma, dma((2,)), dma, dma,
         ],
         compiler_params=pltpu.CompilerParams(
             collective_id=0, has_side_effects=True, vmem_limit_bytes=60 * 1024 * 1024
         ),
     )(*operands)
-    return image.reshape(4, N)
 
 def solution(mesh):
     placed = (

time: 82.9 us -> 79.9 us (0.964)
  Pallas kernels: 81.1 us -> 77.8 us
    pallas_call x1, Pallas kernels: 81.1 us -> 77.8 us  [per_device(): pl.pallas_call(kernel, out_shape=jax.ShapeDtypeStruct((4, N), F32), in_sp...]
    reshape x1 -> x0, local copies, waits for them, and re-layouts: 1.55 us -> none  [per_device(): return image.reshape(4, N)]
    unnamed x0 -> x1, local copies, waits for them, and re-layouts: none -> 1.38 us
where the time goes in v3:
time: 79.9 us; the launch traced here: 79.1 us
  Pallas kernels  77.8 us (97%)
  local copies, waits for them, and re-layouts  1.38 us (2%)
    pallas_call x1, Pallas kernels, per_device(): pl.pallas_call(kernel, out_shape=jax.ShapeDtypeStruct((4, N), F32), in_sp...  77.8 us

profile of v3, /device:TPU:7, one launch (start us, length us, event | category | flops | bytes accessed | tf_op | source)
XLA Modules:
  0.0 79.1 jit_solution(6321310664657300365)
XLA Ops:
  0.0 77.8 %shard_map.109 = f32[4,2048]{1,0:T(4,128)} custom-call(f32[64,2,128]{2,1,0:T(2,128)} %values_hbm.1, s32[64,128]{1,0:T(8,128)} %cell_hbm.1, s32[64,128]{1,0:T(8,128)} %offset_hbm.1, s32[1,64]{1,0:T(1,128)} %bitcast.2, s32[1,64]{1,0:T(1,128)} %bitcast.3, f32[8]{0:T(128)} %depth_hbm.1, bf16[128,768]{1,0:T(8,128)(2,1)} %constant.10.clone.outer_hbm, ...), custom_call_target="tpu_custom_call" | custom-call | tf_op jit(solution)/shard_map/pallas_call | solution.py:462
  77.8 1.4 %copy.13 = f32[4,2048]{1,0:T(4,128)} copy(f32[4,2048]{1,0:T(4,128)} %shard_map.109) | data formatting | bytes 65536

commit v4 on v3

--- a/solution.py
+++ b/solution.py
@@ -26,7 +26,7 @@
 SLOTS = 2 * BANDS // CHUNKS
 GROUP = 8
 ROW_GROUP = 8
-LATE = 8
+HALF = ROWS // 2
 TAP_SCALE = math.sqrt(math.log2(math.e) / (2.0 * SIGMA * SIGMA))
 MESH = pl.DeviceIdType.MESH
 F32 = jnp.float32
@@ -34,11 +34,11 @@
 NN = (((1,), (0,)), ((), ()))
 NT = (((1,), (1,)), ((), ()))
 
-def tier_of(w):
-    return jnp.where((w & 3) == 0, 1 + (w >> 5), 0)
-
 def far_first(n, count):
     return count // 2 + ((n + 1) >> 1) * (1 - 2 * (n & 1))
+
+def near_first(n):
+    return ((n + 2) >> 1) * (1 - 2 * (n & 1))
 
 def halves(x):
     high = x.astype(BF16)
@@ -65,19 +65,24 @@
     r = np.arange(ROWS)
     angle = 2 * np.pi * (q0[:, None] * r[None, :]) / N
     cos, sin = np.cos(angle), np.sin(angle)
+    spans = [slice(HALF, ROWS), slice(0, HALF)]
     turn = np.stack(
-        [np.concatenate([cos, -sin] * 2, axis=1), np.concatenate([sin, cos] * 2, axis=1)]
+        [
+            np.concatenate([a[:, span], b[:, span]] * 4, axis=1)
+            for span in spans
+            for a, b in ((cos, -sin), (sin, cos))
+        ]
     ).astype(np.float32)
     angle = 2 * np.pi * ((r[:, None] * r[None, :]) % ROWS) / ROWS
     cos, sin = np.cos(angle), np.sin(angle)
-    last = np.zeros((2, 2, 2, 2, ROWS, 2, 4, ROWS))
-    for ih in range(2):
-        for il in range(2):
+    last = np.zeros((2, 2, 4, 2, HALF, 2, 4, ROWS))
+    for half in range(2):
+        for i in range(4):
             for c in range(2):
-                last[ih, 0, il, c, :, 0, 2 * ih + il, :] = cos
-                last[ih, 0, il, c, :, 1, 2 * ih + il, :] = sin
-                last[ih, 1, il, c, :, 0, 2 * ih + il, :] = -sin
-                last[ih, 1, il, c, :, 1, 2 * ih + il, :] = cos
+                last[half, 0, i, c, :, 0, i, :] = cos[spans[half]]
+                last[half, 0, i, c, :, 1, i, :] = sin[spans[half]]
+                last[half, 1, i, c, :, 0, i, :] = -sin[spans[half]]
+                last[half, 1, i, c, :, 1, i, :] = cos[spans[half]]
     high, low = host_halves(last.reshape(2, 256, 256))
     final = np.concatenate([high, high, low], axis=1)
     return outer, twist, bands, turn, final
@@ -104,7 +109,7 @@
     values_hbm, cell_hbm, offset_hbm, tile_hbm, band_hbm, depth_hbm,
     outer_hbm, twist_hbm, bands_hbm, turn_hbm, final_hbm, out,
     values, cell, offset, tile, band, depth_ref, outer, twist, bands, turn, final,
-    vis_send, vis_recv, parts, tiles, spec, spill, col_send, col_recv, partial, screen, red_send, red_recv, lines, pairs, ready,
+    vis_send, vis_recv, parts, tiles, spec, spill, col_send, col_recv, partial, screen, red_send, red_recv, lines, pairs,
     load_sem, vis_ssem, vis_rsem, spill_ssem, spill_rsem, col_ssem, col_rsem, red_ssem, red_rsem,
 ):
     g, w = lax.axis_index("layer"), lax.axis_index("uvrow")
@@ -124,15 +129,10 @@
     for load in loads:
         load.start()
 
-    tier = tier_of(w)
-
     @pl.loop(0, BANDS - 1)
     def _(n):
         there = (w + far_first(n, BANDS)) & (BANDS - 1)
-
-        @pl.when(tier_of(there) >= tier)
-        def _():
-            pl.semaphore_signal(barrier, inc=1, device_id={"layer": g, "uvrow": there}, device_id_type=MESH)
+        pl.semaphore_signal(barrier, inc=1, device_id={"layer": g, "uvrow": there}, device_id_type=MESH)
 
     @pl.loop(1, LAYERS)
     def _(i):
@@ -180,19 +180,7 @@
         screen[k, 0] = cos * (1.0 / N)
         screen[k, 1] = sin * (1.0 / N)
 
-    pl.semaphore_wait(barrier, BANDS - 2 * LATE - 1 + LATE * tier + LAYERS - 1)
-
-    @pl.when(tier > 0)
-    def _():
-        @pl.loop(0, BANDS - 1)
-        def _(n):
-            there = (w + far_first(n, BANDS)) & (BANDS - 1)
-
-            @pl.when(tier_of(there) < tier)
-            def _():
-                pl.semaphore_signal(
-                    ready.at[tier - 1], inc=1, device_id={"layer": g, "uvrow": there}, device_id_type=MESH
-                )
+    pl.semaphore_wait(barrier, BANDS - 1 + LAYERS - 1)
 
     def vis_copy(there):
         return pltpu.make_async_remote_copy(
@@ -206,21 +194,7 @@
 
     @pl.loop(0, BANDS - 1)
     def _(n):
-        there = (w + far_first(n, BANDS)) & (BANDS - 1)
-
-        @pl.when(tier_of(there) <= tier)
-        def _():
-            vis_copy(there).start()
-
-    for later in range(2):
-
-        @pl.when(tier <= later)
-        def _():
-            pl.semaphore_wait(ready.at[later], LATE)
-
-            @pl.loop(0, LATE)
-            def _(n):
-                vis_copy(4 * (LATE * later + ((n + z) & (LATE - 1)))).start()
+        vis_copy((w + near_first(n)) & (BANDS - 1)).start()
 
     mine = pl.ds(pl.multiple_of(w * 8, 8), 8)
     pltpu.make_async_copy(vis_send.at[mine], vis_recv.at[mine], vis_rsem.at[w]).start()
@@ -230,10 +204,7 @@
     sublane = lax.broadcasted_iota(jnp.int32, (8, 128), 0)
 
     def source(n):
-        block = n >> 4
-        early = 4 * ((z + n) & 15) + 1 + lax.rem(x + block, 3)
-        late = 4 * ((n & 8) + ((z + n) & 7))
-        return jnp.where(block == 3, late, early)
+        return jnp.where(n == 0, w, (w - near_first(n - 1)) & (BANDS - 1))
 
     def taps(place):
         cell = place >> 3
@@ -332,63 +303,65 @@
         mh, ml = halves(jnp.concatenate([cos, sin], axis=0))
         mix = jnp.where(exact, mh, ml)
 
-        @pl.loop(ROWS, EXT, step=ROW_GROUP)
-        def _(u):
-            for n in range(ROW_GROUP):
-                tile_row(u + n, mix, chunk == 0)
-
+        def tile_rows(first, last):
+            @pl.loop(first, last, step=ROW_GROUP)
+            def _(u):
+                for n in range(ROW_GROUP):
+                    tile_row(u + n, mix, chunk == 0)
+
+        tile_rows(ROWS, EXT)
         if chunk == CHUNKS - 1:
             spill_copy.start()
-
-        @pl.loop(0, ROWS, step=ROW_GROUP)
-        def _(u):
-            for n in range(ROW_GROUP):
-                tile_row(u + n, mix, chunk == 0)
-
-    spill_copy.wait()
-    over = pl.ds(0, (EXT - ROWS) * 16)
-    spec[:, over, :] = spec[:, over, :] + spill[...]
-
-    for ih in range(2):
+        else:
+            tile_rows(0, ROWS)
+
+    for half in range(2):
+        begin = (1 - half) * HALF
+        tile_rows(begin, begin + HALF)
+        if half == 1:
+            spill_copy.wait()
+            over = pl.ds(0, (EXT - ROWS) * 16)
+            spec[:, over, :] = spec[:, over, :] + spill[...]
+
         for dx in range(4):
-            there_x = x ^ dx
+            there_x = (x + dx) & 3
             operand = []
-            for il in range(2):
-                place = pl.ds(4 * there_x + 2 * ih + il, ROWS, stride=16)
+            for i in range(4):
+                place = pl.ds(begin * 16 + 4 * there_x + i, HALF, stride=16)
                 re, im = spec[0, place, :], spec[1, place, :]
                 operand.append(jnp.concatenate([re, -im], axis=1))
                 operand.append(jnp.concatenate([im, re], axis=1))
             oh, ol = halves(jnp.concatenate(operand, axis=0))
-            half = lax.dot_general(
+            rows = lax.dot_general(
                 outer[...], jnp.concatenate([oh, ol, oh], axis=1), NT, preferred_element_type=F32
             )
             for there_z in range(16):
                 at = pl.multiple_of((4 * there_z + there_x) * 8, 8)
-                col_send[ih, pl.ds(at, 8), :] = half[8 * there_z : 8 * there_z + 8]
+                col_send[half, pl.ds(at, 8), :] = rows[8 * there_z : 8 * there_z + 8]
 
             @pl.loop(0, 16 if dx else 15)
             def _(n):
                 there = (((z + far_first(n, 16)) & 15) << 2) + there_x
                 pltpu.make_async_remote_copy(
-                    src_ref=col_send.at[ih, pl.ds(pl.multiple_of(there * 8, 8), 8)],
-                    dst_ref=col_recv.at[ih, pl.ds(pl.multiple_of(w * 8, 8), 8)],
+                    src_ref=col_send.at[half, pl.ds(pl.multiple_of(there * 8, 8), 8)],
+                    dst_ref=col_recv.at[half, pl.ds(pl.multiple_of(w * 8, 8), 8)],
                     send_sem=col_ssem,
-                    recv_sem=col_rsem.at[ih],
+                    recv_sem=col_rsem.at[half],
                     device_id={"layer": g, "uvrow": there},
                     device_id_type=MESH,
                 ).start()
 
     mine = pl.ds(pl.multiple_of(w * 8, 8), 8)
-    for ih in range(2):
-        col_recv[ih, mine, :] = col_send[ih, mine, :]
-
-    def arrived(ih):
-        others = col_recv.at[ih, pl.ds(0, (BANDS - 1) * 8)]
-        pltpu.make_async_copy(others, others, col_rsem.at[ih]).wait()
-
-    def half_image(ih, first, count):
+    for half in range(2):
+        col_recv[half, mine, :] = col_send[half, mine, :]
+
+    def arrived(half):
+        others = col_recv.at[half, pl.ds(0, (BANDS - 1) * 8)]
+        pltpu.make_async_copy(others, others, col_rsem.at[half]).wait()
+
+    def half_image(half, first, count):
         held = jnp.concatenate(
-            [col_recv[ih, pl.ds(first + k, 64, stride=8), :] for k in range(count)], axis=1
+            [col_recv[half, pl.ds(first + k, 64, stride=8), :] for k in range(count)], axis=1
         )
         hh, hl = halves(held)
         both = lax.dot_general(
@@ -398,11 +371,11 @@
         for k in range(count):
             a, b = both[:64, 128 * k : 128 * k + 128], both[64:, 128 * k : 128 * k + 128]
             turned.append(
-                jnp.concatenate([a * turn[0] - b * turn[1], a * turn[1] + b * turn[0]], axis=1)
+                jnp.concatenate([a * turn[2 * half] - b * turn[2 * half + 1], a * turn[2 * half + 1] + b * turn[2 * half]], axis=1)
             )
         th, tl = halves(jnp.concatenate(turned, axis=0))
         return lax.dot_general(
-            jnp.concatenate([th, tl, th], axis=1), final[ih], NN, preferred_element_type=F32
+            jnp.concatenate([th, tl, th], axis=1), final[half], NN, preferred_element_type=F32
         )
 
     arrived(0)
@@ -480,7 +453,6 @@
             pltpu.VMEM((LAYERS, 64, 128), F32),
             pltpu.VMEM((128, 64), F32),
             pltpu.VMEM((64, 128), F32),
-            pltpu.SemaphoreType.REGULAR((2,)),
             dma((len(operands),)), dma, dma((BANDS,)), dma, dma, dma, dma((2,)), dma, dma,
         ],
         compiler_params=pltpu.CompilerParams(

time: 79.9 us -> 69.6 us (0.87)
  the two profiles are of different devices: /device:TPU:7 before, /device:TPU:1 now
where the time goes in v4:
time: 69.6 us; the launch traced here: 69.5 us
  Pallas kernels  68.1 us (98%)
  local copies, waits for them, and re-layouts  1.38 us (2%)
    pallas_call x1, Pallas kernels, per_device(): pl.pallas_call(kernel, out_shape=jax.ShapeDtypeStruct((4, N), F32), in_sp...  68.1 us

profile of v4, /device:TPU:1, one launch (start us, length us, event | category | flops | bytes accessed | tf_op | source)
XLA Modules:
  0.0 69.5 jit_solution(7202483970712450187)
XLA Ops:
  0.0 68.1 %shard_map.109 = f32[4,2048]{1,0:T(4,128)} custom-call(f32[64,2,128]{2,1,0:T(2,128)} %values_hbm.1, s32[64,128]{1,0:T(8,128)} %cell_hbm.1, s32[64,128]{1,0:T(8,128)} %offset_hbm.1, s32[1,64]{1,0:T(1,128)} %bitcast.2, s32[1,64]{1,0:T(1,128)} %bitcast.3, f32[8]{0:T(128)} %depth_hbm.1, bf16[128,768]{1,0:T(8,128)(2,1)} %constant.10.clone.outer_hbm, ...), custom_call_target="tpu_custom_call" | custom-call | tf_op jit(solution)/shard_map/pallas_call | solution.py:435
  68.1 1.4 %copy.13 = f32[4,2048]{1,0:T(4,128)} copy(f32[4,2048]{1,0:T(4,128)} %shard_map.109) | data formatting | bytes 65536

commit v5 on v4

--- a/solution.py
+++ b/solution.py
@@ -24,7 +24,7 @@
 WIDTH = 0.6
 CHUNKS = 2
 SLOTS = 2 * BANDS // CHUNKS
-GROUP = 8
+GROUP = 4
 ROW_GROUP = 8
 HALF = ROWS // 2
 TAP_SCALE = math.sqrt(math.log2(math.e) / (2.0 * SIGMA * SIGMA))
@@ -341,7 +341,7 @@
 
             @pl.loop(0, 16 if dx else 15)
             def _(n):
-                there = (((z + far_first(n, 16)) & 15) << 2) + there_x
+                there = (((z - far_first(n, 16)) & 15) << 2) + there_x
                 pltpu.make_async_remote_copy(
                     src_ref=col_send.at[half, pl.ds(pl.multiple_of(there * 8, 8), 8)],
                     dst_ref=col_recv.at[half, pl.ds(pl.multiple_of(w * 8, 8), 8)],
@@ -434,7 +434,7 @@
     held = [(pltpu.SMEM if a is layer_w else pltpu.VMEM)(a.shape, a.dtype) for a in operands]
     return pl.pallas_call(
         kernel,
-        out_shape=jax.ShapeDtypeStruct((4, N), F32),
+        out_shape=pltpu.VMEM((4, N), F32),
         in_specs=[hbm] * len(operands),
         out_specs=vmem,
         scratch_shapes=[

time: 69.6 us -> 67.9 us (0.976)
  the two profiles are of different devices: /device:TPU:1 before, /device:TPU:7 now
where the time goes in v5:
time: 67.9 us; the launch traced here: 66.8 us
  Pallas kernels  66.1 us (97%)
    pallas_call x1, Pallas kernels, per_device(): pl.pallas_call(kernel, out_shape=pltpu.VMEM((4, N), F32), in_specs=[hbm]...  66.1 us

profile of v5, /device:TPU:7, one launch (start us, length us, event | category | flops | bytes accessed | tf_op | source)
XLA Modules:
  0.0 66.8 jit_solution(16171411283935276404)
XLA Ops:
  0.0 66.1 %shard_map.109 = f32[4,2048]{1,0:T(4,128)S(1)} custom-call(f32[64,2,128]{2,1,0:T(2,128)} %values_hbm.1, s32[64,128]{1,0:T(8,128)} %cell_hbm.1, s32[64,128]{1,0:T(8,128)} %offset_hbm.1, s32[1,64]{1,0:T(1,128)} %bitcast.2, s32[1,64]{1,0:T(1,128)} %bitcast.3, f32[8]{0:T(128)} %depth_hbm.1, bf16[128,768]{1,0:T(8,128)(2,1)} %constant.10.clone.outer_hbm, ...), custom_call_target="tpu_custom_call" | custom-call | tf_op jit(solution)/shard_map/pallas_call | solution.py:435
  66.1 0.6 copy.13

commit v6 on v5

--- a/solution.py
+++ b/solution.py
@@ -20,12 +20,13 @@
 BLOCKS = 64
 ROWS = 32
 EXT = 40
+OVER = K - 1
 SIGMA = 1.45
 WIDTH = 0.6
 CHUNKS = 2
 SLOTS = 2 * BANDS // CHUNKS
 GROUP = 4
-ROW_GROUP = 8
+ROW_GROUP = 16
 HALF = ROWS // 2
 TAP_SCALE = math.sqrt(math.log2(math.e) / (2.0 * SIGMA * SIGMA))
 MESH = pl.DeviceIdType.MESH
@@ -273,7 +274,7 @@
         re = both[:16, :128] - both[16:, 128:]
         im = both[:16, 128:] + both[16:, :128]
         tc, ts = twist[0], twist[1]
-        at = pl.ds(pl.multiple_of(u * 16, 16), 16)
+        at = pl.ds(u * 16 if isinstance(u, int) else pl.multiple_of(u * 16, 16), 16)
         new_re, new_im = re * tc - im * ts, re * ts + im * tc
         if begin:
             spec[0, at, :] = new_re
@@ -284,7 +285,7 @@
 
     after = (w + 1) & (BANDS - 1)
     spill_copy = pltpu.make_async_remote_copy(
-        src_ref=spec.at[:, pl.ds(ROWS * 16, (EXT - ROWS) * 16)],
+        src_ref=spec.at[:, pl.ds(ROWS * 16, OVER * 16)],
         dst_ref=spill,
         send_sem=spill_ssem,
         recv_sem=spill_rsem,
@@ -309,7 +310,8 @@
                 for n in range(ROW_GROUP):
                     tile_row(u + n, mix, chunk == 0)
 
-        tile_rows(ROWS, EXT)
+        for u in range(ROWS, ROWS + OVER):
+            tile_row(u, mix, chunk == 0)
         if chunk == CHUNKS - 1:
             spill_copy.start()
         else:
@@ -320,7 +322,7 @@
         tile_rows(begin, begin + HALF)
         if half == 1:
             spill_copy.wait()
-            over = pl.ds(0, (EXT - ROWS) * 16)
+            over = pl.ds(0, OVER * 16)
             spec[:, over, :] = spec[:, over, :] + spill[...]
 
         for dx in range(4):
@@ -444,7 +446,7 @@
             pltpu.VMEM((SLOTS * 2 * EXT, 128), F32),
             pltpu.VMEM((max(128, 3 * SLOTS), 128), F32),
             pltpu.VMEM((2, EXT * 16, 128), F32),
-            pltpu.VMEM((2, (EXT - ROWS) * 16, 128), F32),
+            pltpu.VMEM((2, OVER * 16, 128), F32),
             pltpu.VMEM((2, BANDS * 8, 128), F32),
             pltpu.VMEM((2, BANDS * 8, 128), F32),
             pltpu.VMEM((LAYERS * 64, 256), F32),

time: 67.9 us -> 67.6 us (level)
  the two profiles are of different devices: /device:TPU:7 before, /device:TPU:1 now
where the time goes in v6:
time: 67.6 us; the launch traced here: 67.5 us
  Pallas kernels  66.9 us (99%)
    pallas_call x1, Pallas kernels, per_device(): pl.pallas_call(kernel, out_shape=pltpu.VMEM((4, N), F32), in_specs=[hbm]...  66.9 us

profile of v6, /device:TPU:1, one launch (start us, length us, event | category | flops | bytes accessed | tf_op | source)
XLA Modules:
  0.0 67.5 jit_solution(16414560228732838293)
XLA Ops:
  0.0 66.9 %shard_map.109 = f32[4,2048]{1,0:T(4,128)S(1)} custom-call(f32[64,2,128]{2,1,0:T(2,128)} %values_hbm.1, s32[64,128]{1,0:T(8,128)} %cell_hbm.1, s32[64,128]{1,0:T(8,128)} %offset_hbm.1, s32[1,64]{1,0:T(1,128)} %bitcast.2, s32[1,64]{1,0:T(1,128)} %bitcast.3, f32[8]{0:T(128)} %depth_hbm.1, bf16[128,768]{1,0:T(8,128)(2,1)} %constant.10.clone.outer_hbm, ...), custom_call_target="tpu_custom_call" | custom-call | tf_op jit(solution)/shard_map/pallas_call | solution.py:437
  66.9 0.6 copy.13
